TPU v7x, 256 devices: a whole 4x4x8 slice. The times are simulated.
256 devices in a mesh: section: 2 (over core), diam: 128 (over x, z, y).
Axes of the slice: x: 4, y: 4, z: 8, core: 2. Of those that a mesh axis runs over, the one named last changes fastest.
Arguments:
- modal: bfloat16 [2, 256, 19, 512, 128], P('section', 'diam'), may hold values from -6 to 6
- stiffness: bfloat16 [2, 256, 512, 512], P('section', 'diam'), may hold values from -0.25 to 0.25
- mass: bfloat16 [2, 256, 512, 512], P('section', 'diam'), may hold values from -0.25 to 0.25
- freq: float32 [128], replicated, may hold values from 0.02 to 0.11
- coupling: bfloat16 [2, 256, 4, 32, 32], P('section', 'diam'), may hold values from -1 to 1
- route: int32 [2, 19456, 1], P('section', 'diam'), may hold values from 0 to 127; in each aligned block of 152 rows (0 to 151, 152 to 303, ..., all dimensions but the last counted through in order) at most 2 rows name the same one
- target: int32 [2, 19456], P('section', 'diam'), may hold values from 0 to 151
- contact_dof: int32 [2, 16384], P('section', 'diam'), may hold values from 0 to 511
- evaluator: int32 [2, 16384, 1], P('section', 'diam'), may hold values from 0 to 127; in each aligned block of 128 rows (0 to 127, 128 to 255, ..., all dimensions but the last counted through in order) at most 2 rows name the same one
- preload: bfloat16 [2, 16384], P('section', 'diam'), may hold values from 0.5 to 13.5, as said below
Outputs:
- residual: bfloat16 [2, 256, 19, 512, 128], P('section', 'diam')
Inputs may be any that keep to these rules, and one draw needn't show every extreme that they name: `route`: destination device of each tile on the other section; among the tiles of one device no destination appears more than 2 times, a bound that some block reaches; every destination appears. `evaluator`: joint of each row, one joint to each index of diam in the same section; among the rows of one device no joint appears more than 2 times, a bound that some block reaches; every joint has rows. `preload`: positive.
All inputs are finite; a program needn't handle non-finite values.
Results may differ from a plain program's by a relative error of at most 0.0028.
Values may be sent and summed in bfloat16 or wider, within the bound.
A program may use at most 128 MiB of HBM per device.

v0:
```python
import math

import jax
import jax.numpy as jnp
from jax import lax
from jax.sharding import PartitionSpec as P

HARM = 9
NCOMP = 19
NIF = 128
NPATCH = 4
NIFP = 32
NT = 128


JOINT_STIFFNESS = 0.3
FRICTION = 0.6
SMOOTHING = 0.1


def swapped(array, axis, apart):
    return lax.ppermute(array, axis, [(i, i ^ 1 << apart) for i in range(lax.axis_size(axis))])


def harmonic_order():
    comp_index = jnp.arange(NCOMP)
    return jnp.where(comp_index <= HARM, comp_index, comp_index - HARM).astype(jnp.float32)


def time_tables():
    comp_index = jnp.arange(NCOMP)
    harm_order = harmonic_order()
    tau_grid = jnp.arange(NT).astype(jnp.float32) * (2.0 * math.pi / NT)
    phase = harm_order[:, None] * tau_grid[None, :]
    is_sine = (comp_index > HARM)[:, None]
    slope_table = jnp.where(
        is_sine, harm_order[:, None] * jnp.cos(phase), -harm_order[:, None] * jnp.sin(phase)
    )
    shape_table = jnp.where(is_sine, jnp.sin(phase), jnp.cos(phase))
    weights = jnp.where(comp_index == 0, 1.0 / NT, 2.0 / NT).astype(jnp.float32)
    projection = jnp.transpose(shape_table * weights[:, None])
    return (slope_table, projection)


def joint_forces(payload, pressure, joint_mean, freq, slope_table, projection):
    coefficient = payload.astype(jnp.float32)
    velocity = freq[None, None, :, None] * jnp.einsum(
        "scjp,ct->sjpt", coefficient, slope_table, precision=lax.Precision.HIGHEST
    )
    slip_speed = jnp.sqrt(velocity[:, 0] ** 2 + velocity[:, 1] ** 2 + SMOOTHING**2)
    sliding = FRICTION * pressure[:, None, None, None] * velocity / slip_speed[:, None]
    harmonic = jnp.einsum("sjpt,tc->scjp", sliding, projection, precision=lax.Precision.HIGHEST)
    return (JOINT_STIFFNESS * (coefficient - joint_mean) + harmonic).astype(jnp.bfloat16)


def slot_positions(destination, width, depth):
    hit_table = (destination[:, None] == jnp.arange(width)[None, :]).astype(jnp.int32)
    earlier = jnp.cumsum(hit_table, axis=0) - hit_table
    return destination * depth + jnp.sum(earlier * hit_table, axis=1)


def block_rows(row_count):
    size_rows = 64
    while row_count % size_rows:
        size_rows = size_rows // 2
    return size_rows


def evaluate_rows(payload, pressure, joint_mean, freq):
    slope_table, projection = time_tables()
    row_count = payload.shape[0]
    step_rows = block_rows(row_count)
    turns = row_count // step_rows

    def on_block(packed_args):
        return joint_forces(
            packed_args[0], packed_args[1], packed_args[2], freq, slope_table, projection
        )

    shaped = (
        payload.reshape((turns, step_rows) + payload.shape[1:]),
        pressure.reshape(turns, step_rows),
        joint_mean.reshape((turns, step_rows) + joint_mean.shape[1:]),
    )
    return lax.map(on_block, shaped).reshape(payload.shape)


def body(modal, stiffness, mass, freq, coupling, route, target, contact_dof, evaluator, preload):
    width = lax.axis_size("diam")
    field = modal[0]
    block_total, comp_total, dof_total, point_total = field.shape
    half_dof = dof_total // 2
    tiles_dev = block_total * comp_total * NPATCH
    depth_tiles = max(2, 2 * tiles_dev // width)
    omega_square = (harmonic_order()[:, None] * freq[None, :]) ** 2
    stiff_part = jnp.einsum(
        "bcdp,bde->bcep", field, stiffness[0], preferred_element_type=jnp.float32
    )
    inertia = jnp.einsum("bcdp,bde->bcep", field, mass[0], preferred_element_type=jnp.float32)
    send_tiles = field[:, :, :NIF, :].reshape(tiles_dev, NIFP, point_total)
    destination = route[0, :, 0]
    slot_target = target[0]
    where_to = slot_positions(destination, width, depth_tiles)
    packed = (
        jnp.zeros((width * depth_tiles, NIFP, point_total), jnp.bfloat16)
        .at[where_to]
        .set(send_tiles)
    )
    slot_tags = jnp.zeros((width * depth_tiles,), jnp.int32).at[where_to].set(slot_target)
    arrived, arrived_tags = (
        lax.all_to_all(
            packed.reshape(width, depth_tiles, NIFP, point_total),
            "diam",
            split_axis=0,
            concat_axis=0,
            tiled=True,
        ),
        lax.all_to_all(
            slot_tags.reshape(width, depth_tiles), "diam", split_axis=0, concat_axis=0, tiled=True
        ),
    )
    arrived, arrived_tags = swapped((arrived, arrived_tags), "section", 0)
    selector = (
        arrived_tags.reshape(1, width * depth_tiles) == jnp.arange(tiles_dev)[:, None]
    ).astype(jnp.bfloat16)
    glued = jnp.dot(
        selector,
        arrived.reshape(width * depth_tiles, NIFP * point_total),
        preferred_element_type=jnp.float32,
    ).astype(jnp.bfloat16)
    glued = glued.reshape(block_total, comp_total, NPATCH, NIFP, point_total)
    dof_list = contact_dof[0]
    block_index = dof_list // half_dof
    dof_pair = dof_list % half_dof
    by_pairs = field.reshape(block_total, comp_total, half_dof, 2, point_total)
    payload = by_pairs[block_index[:, None], jnp.arange(comp_total)[None, :], dof_pair[:, None]]
    preloads = preload[0]
    joint_index = evaluator[0, :, 0]
    row_total = dof_list.shape[0]
    depth_rows = max(2, 2 * row_total // width)
    slots = slot_positions(joint_index, width, depth_rows)
    send_payload = (
        jnp.zeros((width * depth_rows, comp_total, 2, point_total), jnp.bfloat16)
        .at[slots]
        .set(payload)
    )
    send_load = jnp.zeros((width * depth_rows,), jnp.bfloat16).at[slots].set(preloads)
    got_payload, got_load = (
        lax.all_to_all(
            send_payload.reshape(width, depth_rows, comp_total, 2, point_total),
            "diam",
            split_axis=0,
            concat_axis=0,
            tiled=True,
        ),
        lax.all_to_all(
            send_load.reshape(width, depth_rows), "diam", split_axis=0, concat_axis=0, tiled=True
        ),
    )
    got_payload = got_payload.reshape(width * depth_rows, comp_total, 2, point_total)
    load_wide = got_load.reshape(width * depth_rows).astype(jnp.float32)
    joint_load = jnp.sum(load_wide)
    weighted = jnp.dot(
        load_wide[None, :],
        got_payload.reshape(width * depth_rows, comp_total * 2 * point_total).astype(jnp.float32),
        precision=lax.Precision.HIGHEST,
    )
    joint_mean = (weighted / joint_load).reshape(1, comp_total, 2, point_total)
    pressure = load_wide * row_total / joint_load
    computed = evaluate_rows(
        got_payload, pressure, jnp.broadcast_to(joint_mean, got_payload.shape), freq
    )
    returned = lax.all_to_all(
        computed.reshape(width, depth_rows, comp_total, 2, point_total),
        "diam",
        split_axis=0,
        concat_axis=0,
        tiled=True,
    )
    contact_force = returned.reshape(width * depth_rows, comp_total, 2, point_total)[slots]
    residual = stiff_part - omega_square[None, :, None, :] * inertia
    linkage = jnp.einsum(
        "bcqip,bqij->bcqjp", glued, coupling[0], preferred_element_type=jnp.float32
    )
    residual = residual.at[:, :, :NIF, :].add(
        linkage.reshape(block_total, comp_total, NIF, point_total)
    )
    split_rows = residual.reshape(block_total, comp_total, half_dof, 2, point_total)
    split_rows = split_rows.at[
        block_index[:, None], jnp.arange(comp_total)[None, :], dof_pair[:, None]
    ].add(contact_force.astype(jnp.float32))
    return split_rows.reshape(1, block_total, comp_total, dof_total, point_total).astype(
        jnp.bfloat16
    )


def solution(mesh):
    placed = (
        P("section", "diam", None, None, None),
        P("section", "diam", None, None),
        P("section", "diam", None, None),
        P(),
        P("section", "diam", None, None, None),
        P("section", "diam", None),
        P("section", "diam"),
        P("section", "diam"),
        P("section", "diam", None),
        P("section", "diam"),
    )
    return jax.shard_map(
        body,
        mesh=mesh,
        in_specs=placed,
        out_specs=P("section", "diam", None, None, None),
        check_vma=False,
    )
```

profile of v0, /device:TPU:4, one launch (start us, length us, event | category | flops | bytes accessed | tf_op | source)
XLA Modules:
  0.0 586.5 jit_solution(6623275269324568180)
XLA Ops:
  2.5 1.5 scatter_custom_fusion.3
  4.8 16.2 %all-to-all-start.3 = ((bf16[128,1,2]{2,1,0:T(2,128)(2,1)}), bf16[128,1,2]{2,1,0:T(2,128)(2,1)}, u32[]{:S(2)}, u32[]{:S(2)}) async-start(bf16[128,1,2]{2,1,0:T(2,128)(2,1)} %all_to_all.31), calls=%async_computation.3 | async-start | bytes 131072 | tf_op jit(solution)/shard_map/all_to_all | solution.py:156
  22.6 36.3 %gather_fusion = bf16[2432,2,128]{2,1,0:T(2,128)(2,1)} fusion(bf16[2,19,256,2,128]{4,3,2,1,0:T(2,128)(2,1)} %bitcast.165, s32[2432]{0:T(1024)S(1)} %reshape.333), kind=kCustom, calls=%fused_computation | custom fusion | bytes 2519552 | tf_op jit(solution)/shard_map/gather | solution.py:136
  60.2 11.6 %scatter_fusion.1 = bf16[256,19,2,128]{3,2,1,0:T(2,128)(2,1)S(1)} fusion(bf16[256,19,2,128]{3,2,1,0:T(2,128)(2,1)S(1)} %broadcast_in_dim.48, s32[128]{0:T(128)S(1)} %fusion.62, bf16[128,19,2,128]{3,2,1,0:T(2,128)(2,1)} %bitcast.174), kind=kCustom, calls=%fused_computation.4 | custom fusion | bytes 3736064 | tf_op jit(solution)/shard_map/scatter | solution.py:145
  71.8 1.4 copy-done.1
  73.2 13.9 %all-to-all-start.2 = ((bf16[128,2,19,2,128]{4,3,2,1,0:T(2,128)(2,1)}), bf16[128,2,19,2,128]{4,3,2,1,0:T(2,128)(2,1)S(1)}, u32[]{:S(2)}, u32[]{:S(2)}) async-start(bf16[128,2,19,2,128]{4,3,2,1,0:T(2,128)(2,1)} %bitcast.170), calls=%async_computation.2 | async-start | bytes 4980736 | tf_op jit(solution)/shard_map/all_to_all | solution.py:149
  89.1 2.5 slice.66
  93.7 1.6 broadcast_in_dim.41
  95.4 19.0 %scatter_fusion = bf16[256,32,128]{2,1,0:T(8,128)(2,1)} fusion(bf16[256,32,128]{2,1,0:T(8,128)(2,1)} %broadcast_in_dim.41, s32[152]{0:T(256)S(1)} %bitcast.186, bf16[152,32,128]{2,1,0:T(8,128)(2,1)} %bitcast.173), kind=kCustom, calls=%fused_computation.3 | custom fusion | bytes 3736160 | tf_op jit(solution)/shard_map/scatter | solution.py:107
  118.5 1.3 fusion.60
  119.9 1.6 reduce.6
  121.5 1.5 reshape.390
  123.0 1.7 convert_reduce_fusion
  124.6 2.4 divide_reduce_fusion
  127.0 1.5 div.47
  128.5 16.8 %all-to-all-done.2 = bf16[128,2,19,2,128]{4,3,2,1,0:T(2,128)(2,1)S(1)} async-done(((bf16[128,2,19,2,128]{4,3,2,1,0:T(2,128)(2,1)}), bf16[128,2,19,2,128]{4,3,2,1,0:T(2,128)(2,1)S(1)}, u32[]{:S(2)}, u32[]{:S(2)}) %all-to-all-start.2) | async-done | bytes 2490400 | tf_op jit(solution)/shard_map/all_to_all | solution.py:149
  145.3 9.8 %all-to-all-start = ((s32[128,1,2]{2,1,0:T(1,128)}), s32[128,1,2]{2,1,0:T(1,128)}, u32[]{:S(2)}, u32[]{:S(2)}) async-start(s32[128,1,2]{2,1,0:T(1,128)} %bitcast.180), calls=%async_computation | async-start | bytes 131072 | tf_op jit(solution)/shard_map/all_to_all | solution.py:118
  155.1 2.5 reshape_reshape.10
  157.6 2.2 convolution_reduce_fusion
  161.0 1.3 broadcast_in_dim.54
  162.4 1.3 copy.52
  163.7 2.2 copy.50
  165.9 14.7 %all-to-all-start.1 = ((bf16[128,2,32,128]{3,2,1,0:T(8,128)(2,1)}), bf16[128,2,32,128]{3,2,1,0:T(8,128)(2,1)}, u32[]{:S(2)}, u32[]{:S(2)}) async-start(bf16[128,2,32,128]{3,2,1,0:T(8,128)(2,1)} %bitcast.171), calls=%async_computation.1 | async-start | bytes 4194304 | tf_op jit(solution)/shard_map/all_to_all | solution.py:111
  180.7 3.1 reshape.323
  183.9 76.7 %while.13 = (s32[]{:T(128)}, bf16[4,64,19,2,128]{4,2,3,1,0:T(8,128)(2,1)}, bf16[4,64,19,2,128]{4,2,3,1,0:T(8,128)(2,1)}, f32[4,64,19,2,128]{4,2,3,1,0:T(8,128)},...) while((s32[]{:T(128)}, ...), condition=%wide.region_11.12_spmd.clone.clone, body=%wide.region_10.11_spmd.clone.clone.sunk | while | flops 968360640 | bytes 37490384 | solution.py:85
  183.9 6.8 %broadcast_multiply_fusion.2 = f32[64,2,128,128]{3,2,1,0:T(8,128)S(1)} fusion(f32[128]{0:T(128)S(1)} %get-tuple-element.256, bf16[4,64,19,2,128]{4,2,3,1,0:T(8,128)(2,1)} %get-tuple-element.253, s32[]{:T(128)} %get-tuple-element.239, f32[19]{0:T(128)S(1)} %get-tuple-element.259, f32[128]{0:T(128)S(1)} %get-tuple-element.257, ...), kind=kOutput, calls=%fused_computation.18.clone.1 | convolution fusion | flops 480257536 | bytes 9176747 | tf_op jit(solution)/shard_map/while/body/eval_jaxpr/scjp,ct->sjpt/dot_general | solution.py:47
  190.7 1.5 fusion.81
  193.0 10.1 %fusion.83 = bf16[4,64,19,2,128]{4,2,3,1,0:T(8,128)(2,1)} fusion(bf16[4,64,19,2,128]{4,2,3,1,0:T(8,128)(2,1)} %get-tuple-element.240, s32[]{:T(128)} %get-tuple-element.239, f32[64,2,128,128]{3,2,1,0:T(8,128)S(1)} %broadcast_multiply_fusion.2, f32[64,128,128]{2,1,0:T(8,128)S(1)} %fusion.81, f32[64]{0:T(128)S(1)} %fusion.82, ...), kind=kOutput, calls=%fused_computation.25.clone.1 | convolution fusion | flops 483908736 | bytes 15730091 | tf_op jit(solution)/shard_map/while/body/eval_jaxpr/sjpt,tc->scjp/dot_general | solution.py:52
  203.0 6.8 %broadcast_multiply_fusion.2 = f32[64,2,128,128]{3,2,1,0:T(8,128)S(1)} fusion(f32[128]{0:T(128)S(1)} %get-tuple-element.256, bf16[4,64,19,2,128]{4,2,3,1,0:T(8,128)(2,1)} %get-tuple-element.253, s32[]{:T(128)} %get-tuple-element.239, f32[19]{0:T(128)S(1)} %get-tuple-element.259, f32[128]{0:T(128)S(1)} %get-tuple-element.257, ...), kind=kOutput, calls=%fused_computation.18.clone.1 | convolution fusion | flops 480257536 | bytes 9176747 | tf_op jit(solution)/shard_map/while/body/eval_jaxpr/scjp,ct->sjpt/dot_general | solution.py:47
  209.8 1.5 fusion.81
  212.1 10.1 %fusion.83 = bf16[4,64,19,2,128]{4,2,3,1,0:T(8,128)(2,1)} fusion(bf16[4,64,19,2,128]{4,2,3,1,0:T(8,128)(2,1)} %get-tuple-element.240, s32[]{:T(128)} %get-tuple-element.239, f32[64,2,128,128]{3,2,1,0:T(8,128)S(1)} %broadcast_multiply_fusion.2, f32[64,128,128]{2,1,0:T(8,128)S(1)} %fusion.81, f32[64]{0:T(128)S(1)} %fusion.82, ...), kind=kOutput, calls=%fused_computation.25.clone.1 | convolution fusion | flops 483908736 | bytes 15730091 | tf_op jit(solution)/shard_map/while/body/eval_jaxpr/sjpt,tc->scjp/dot_general | solution.py:52
  222.2 6.8 %broadcast_multiply_fusion.2 = f32[64,2,128,128]{3,2,1,0:T(8,128)S(1)} fusion(f32[128]{0:T(128)S(1)} %get-tuple-element.256, bf16[4,64,19,2,128]{4,2,3,1,0:T(8,128)(2,1)} %get-tuple-element.253, s32[]{:T(128)} %get-tuple-element.239, f32[19]{0:T(128)S(1)} %get-tuple-element.259, f32[128]{0:T(128)S(1)} %get-tuple-element.257, ...), kind=kOutput, calls=%fused_computation.18.clone.1 | convolution fusion | flops 480257536 | bytes 9176747 | tf_op jit(solution)/shard_map/while/body/eval_jaxpr/scjp,ct->sjpt/dot_general | solution.py:47
  229.0 1.5 fusion.81
  231.2 10.1 %fusion.83 = bf16[4,64,19,2,128]{4,2,3,1,0:T(8,128)(2,1)} fusion(bf16[4,64,19,2,128]{4,2,3,1,0:T(8,128)(2,1)} %get-tuple-element.240, s32[]{:T(128)} %get-tuple-element.239, f32[64,2,128,128]{3,2,1,0:T(8,128)S(1)} %broadcast_multiply_fusion.2, f32[64,128,128]{2,1,0:T(8,128)S(1)} %fusion.81, f32[64]{0:T(128)S(1)} %fusion.82, ...), kind=kOutput, calls=%fused_computation.25.clone.1 | convolution fusion | flops 483908736 | bytes 15730091 | tf_op jit(solution)/shard_map/while/body/eval_jaxpr/sjpt,tc->scjp/dot_general | solution.py:52
  241.3 6.8 %broadcast_multiply_fusion.2 = f32[64,2,128,128]{3,2,1,0:T(8,128)S(1)} fusion(f32[128]{0:T(128)S(1)} %get-tuple-element.256, bf16[4,64,19,2,128]{4,2,3,1,0:T(8,128)(2,1)} %get-tuple-element.253, s32[]{:T(128)} %get-tuple-element.239, f32[19]{0:T(128)S(1)} %get-tuple-element.259, f32[128]{0:T(128)S(1)} %get-tuple-element.257, ...), kind=kOutput, calls=%fused_computation.18.clone.1 | convolution fusion | flops 480257536 | bytes 9176747 | tf_op jit(solution)/shard_map/while/body/eval_jaxpr/scjp,ct->sjpt/dot_general | solution.py:47
  248.1 1.5 fusion.81
  250.3 10.1 %fusion.83 = bf16[4,64,19,2,128]{4,2,3,1,0:T(8,128)(2,1)} fusion(bf16[4,64,19,2,128]{4,2,3,1,0:T(8,128)(2,1)} %get-tuple-element.240, s32[]{:T(128)} %get-tuple-element.239, f32[64,2,128,128]{3,2,1,0:T(8,128)S(1)} %broadcast_multiply_fusion.2, f32[64,128,128]{2,1,0:T(8,128)S(1)} %fusion.81, f32[64]{0:T(128)S(1)} %fusion.82, ...), kind=kOutput, calls=%fused_computation.25.clone.1 | convolution fusion | flops 483908736 | bytes 15730091 | tf_op jit(solution)/shard_map/while/body/eval_jaxpr/sjpt,tc->scjp/dot_general | solution.py:52
  260.6 5.9 %copy.53 = bf16[128,2,19,2,128]{4,3,2,1,0:T(2,128)(2,1)} copy(bf16[128,2,19,2,128]{4,2,3,1,0:T(8,128)(2,1)} %bitcast.34) | data formatting | bytes 4980736 | tf_op jit(solution)/shard_map/reshape;reshape | solution.py:174
  266.5 14.3 %all-to-all-start.4 = ((bf16[128,2,19,2,128]{4,3,2,1,0:T(2,128)(2,1)}), bf16[128,2,19,2,128]{4,3,2,1,0:T(2,128)(2,1)}, u32[]{:S(2)}, u32[]{:S(2)}) async-start(bf16[128,2,19,2,128]{4,3,2,1,0:T(2,128)(2,1)} %copy.53), calls=%async_computation.4 | async-start | bytes 4980736 | tf_op jit(solution)/shard_map/all_to_all | solution.py:173
  281.1 5.2 fusion.46
  286.5 5.5 subtract_bitcast_fusion
  293.9 2.5 fusion.41
  297.5 3.6 fusion.38
  301.1 36.4 %all-to-all-done.4 = bf16[128,2,19,2,128]{4,3,2,1,0:T(2,128)(2,1)} async-done(((bf16[128,2,19,2,128]{4,3,2,1,0:T(2,128)(2,1)}), bf16[128,2,19,2,128]{4,3,2,1,0:T(2,128)(2,1)}, u32[]{:S(2)}, u32[]{:S(2)}) %all-to-all-start.4) | async-done | bytes 2490400 | tf_op jit(solution)/shard_map/all_to_all | solution.py:173
  337.4 5.8 gather_fusion.1
  343.2 2.6 bitcast_convert_fusion
  345.8 233.5 %scatter_fusion.2 = f32[9728,2,128]{2,1,0:T(2,128)} fusion(f32[9728,2,128]{2,1,0:T(2,128)} %bitcast.23, s32[2432]{0:T(1024)S(1)} %reshape.379, f32[2432,2,128]{2,1,0:T(2,128)S(1)} %bitcast_convert_fusion), kind=kCustom, calls=%fused_computation.6 | custom fusion | flops 622592 | bytes 7480832
  579.3 6.9 %convert_element_type.75 = bf16[9728,2,128]{2,1,0:T(2,128)(2,1)} convert(f32[9728,2,128]{2,1,0:T(2,128)} %scatter_fusion.2) | non-fusion elementwise | flops 2490368 | bytes 14942208 | tf_op jit(solution)/shard_map/convert_element_type | solution.py:192
  (97 shorter events, 21.7 us)
Async XLA Ops:
  0.0 281.1 %copy-start = (bf16[1,2,512,512]{3,2,1,0:T(8,128)(2,1)S(1)}, bf16[1,2,512,512]{3,2,1,0:T(8,128)(2,1)}, u32[]{:S(2)}) copy-start(bf16[1,2,512,512]{3,2,1,0:T(8,128)(2,1)} %param.15) | copy-start | bytes 3145732
  2.5 57.7 %copy-start.16 = (s32[128]{0:T(128)}, s32[128]{0:T(128)S(1)}, u32[]{:S(2)}) copy-start(s32[128]{0:T(128)S(1)} %fusion.62) | copy-start | bytes 1540
  4.8 67.0 %all-to-all-start.3 = ((bf16[128,1,2]{2,1,0:T(2,128)(2,1)}), bf16[128,1,2]{2,1,0:T(2,128)(2,1)}, u32[]{:S(2)}, u32[]{:S(2)}) async-start(bf16[128,1,2]{2,1,0:T(2,128)(2,1)} %all_to_all.31), calls=%async_computation.3 | async-start | bytes 131072 | tf_op jit(solution)/shard_map/all_to_all | solution.py:156
  71.8 1.4 copy-start.1
  73.2 13.9 %copy-start.15 = (s32[1,152,1]{1,2,0:T(1,128)S(1)}, s32[1,152,1]{1,2,0:T(1,128)}, u32[]{:S(2)}) copy-start(s32[1,152,1]{1,2,0:T(1,128)} %param.19) | copy-start | bytes 1828
  73.2 72.1 %all-to-all-start.2 = ((bf16[128,2,19,2,128]{4,3,2,1,0:T(2,128)(2,1)}), bf16[128,2,19,2,128]{4,3,2,1,0:T(2,128)(2,1)S(1)}, u32[]{:S(2)}, u32[]{:S(2)}) async-start(bf16[128,2,19,2,128]{4,3,2,1,0:T(2,128)(2,1)} %bitcast.170), calls=%async_computation.2 | async-start | bytes 4980736 | tf_op jit(solution)/shard_map/all_to_all | solution.py:149
  87.4 0.7 copy-start.3
  117.3 0.6 copy-start.4
  117.9 0.6 copy-start.6
  145.3 20.6 %all-to-all-start = ((s32[128,1,2]{2,1,0:T(1,128)}), s32[128,1,2]{2,1,0:T(1,128)}, u32[]{:S(2)}, u32[]{:S(2)}) async-start(s32[128,1,2]{2,1,0:T(1,128)} %bitcast.180), calls=%async_computation | async-start | bytes 131072 | tf_op jit(solution)/shard_map/all_to_all | solution.py:118
  165.9 14.8 %copy-start.8 = (f32[19,2,128]{2,0,1:T(8,128)S(1)}, f32[19,2,128]{2,0,1:T(8,128)}, u32[]{:S(2)}) copy-start(f32[19,2,128]{2,0,1:T(8,128)} %copy.52) | copy-start | bytes 58372
  165.9 100.6 %all-to-all-start.1 = ((bf16[128,2,32,128]{3,2,1,0:T(8,128)(2,1)}), bf16[128,2,32,128]{3,2,1,0:T(8,128)(2,1)}, u32[]{:S(2)}, u32[]{:S(2)}) async-start(bf16[128,2,32,128]{3,2,1,0:T(8,128)(2,1)} %bitcast.171), calls=%async_computation.1 | async-start | bytes 4194304 | tf_op jit(solution)/shard_map/all_to_all | solution.py:111
  180.7 3.2 copy-start.10
  180.7 3.2 copy-start.11
  180.7 3.2 copy-start.12
  180.7 3.2 copy-start.13
  180.7 3.2 copy-start.19
  266.5 14.4 %copy-start.5 = (s32[128,19,1]{0,1,2:T(8,128)S(1)}, s32[128,19,1]{0,1,2:T(8,128)}, u32[]{:S(2)}) copy-start(s32[128,19,1]{0,1,2:T(8,128)} %copy-done.4) | copy-start | bytes 29188
  266.5 14.4 %copy-start.7 = (s32[128,19,1]{0,1,2:T(8,128)S(1)}, s32[128,19,1]{0,1,2:T(8,128)}, u32[]{:S(2)}) copy-start(s32[128,19,1]{0,1,2:T(8,128)} %copy-done.6) | copy-start | bytes 29188
  266.5 14.4 %copy-start.18 = (s32[3]{0:T(128)S(1)}, s32[3]{0:T(128)}, u32[]{:S(2)}) copy-start(s32[3]{0:T(128)} %constant.129) | copy-start | bytes 40
  266.5 14.6 %copy-start.14 = (pred[128,19]{0,1:T(8,128)(4,1)S(1)}, pred[128,19]{0,1:T(8,128)(4,1)}, u32[]{:S(2)}) copy-start(pred[128,19]{0,1:T(8,128)(4,1)} %fusion.60) | copy-start | bytes 7300
  266.5 19.9 %slice-start = ((s8[4980736]{0:T(1024)(128)(4,1)}), s8[786432]{0:T(1024)(128)(4,1)S(1)}, s32[]{:S(2)}) async-start(s8[4980736]{0:T(1024)(128)(4,1)} %bitcast.167), calls=%async_computation.5 | async-start | bytes 1572864
  266.5 70.9 %all-to-all-start.4 = ((bf16[128,2,19,2,128]{4,3,2,1,0:T(2,128)(2,1)}), bf16[128,2,19,2,128]{4,3,2,1,0:T(2,128)(2,1)}, u32[]{:S(2)}, u32[]{:S(2)}) async-start(bf16[128,2,19,2,128]{4,3,2,1,0:T(2,128)(2,1)} %copy.53), calls=%async_computation.4 | async-start | bytes 4980736 | tf_op jit(solution)/shard_map/all_to_all | solution.py:173
  281.1 5.4 slice-start.1
  281.1 5.4 copy-start.2
  286.3 6.3 %copy-start.17 = (s32[128]{0:T(128)S(1)}, s32[128]{0:T(128)}, u32[]{:S(2)}) copy-start(s32[128]{0:T(128)} %copy-done.16) | copy-start | bytes 1540
  286.3 7.5 %collective-permute-start.1 = (bf16[128,2,32,128]{3,2,1,0:T(8,128)(2,1)}, bf16[128,2,32,128]{3,2,1,0:T(8,128)(2,1)}, u32[]{:S(2)}, u32[]{:S(2)}) collective-permute-start(bf16[128,2,32,128]{3,2,1,0:T(8,128)(2,1)} %all-to-all-done.1), channel_id=1, source_target_pairs={{0,128},{128,0},{1,129},{129,1},{2,130},{130,2},{3,131},{131,3},{4... | collective-permute-start | bytes 6291464 | tf_op jit(solution)/shard_map/ppermute | solution.py:22
  291.9 1.8 collective-permute-start
  293.9 2.8 copy-start.9
where the time goes:
time: 595 us; the launch traced here: 586 us
  other arithmetic  271 us (46%)
  local copies, waits for them, and re-layouts  108 us (18%)
  matrix products  83.4 us (14%)
  starting transfers between devices  69.8 us (12%)
  waiting for transfers between devices  53.9 us (9%)
    unnamed x5, other arithmetic  235 us
    dot_general x4, matrix products, joint_forces(): jnp.einsum('sjpt,tc->scjp', sliding, projection, precision=lax.Precision....  40.4 us
    all_to_all x1, waiting for transfers between devices, body(): lax.all_to_all(computed.reshape(width, depth_rows, comp_total, 2, point_t...  36.4 us
    gather x1, local copies, waits for them, and re-layouts, body(): by_pairs[block_index[:, None], jnp.arange(comp_total)[None, :], dof_pair[...  36.3 us
    dot_general x4, matrix products, joint_forces(): jnp.einsum('scjp,ct->sjpt', coefficient, slope_table, precision=lax.Preci...  27.2 us
    scatter x1, local copies, waits for them, and re-layouts, body(): packed = jnp.zeros((width * depth_tiles, NIFP, point_total), jnp.bfloat16...  19 us
    all_to_all x1, waiting for transfers between devices, body(): lax.all_to_all(send_payload.reshape(width, depth_rows, comp_total, 2, poi...  16.8 us
    all_to_all x1, starting transfers between devices, body(): lax.all_to_all(send_load.reshape(width, depth_rows), 'diam', split_axis=0...  16.2 us
  transfers between devices with their start and end apart: 7, of which 3 were waited for; matrix products, arithmetic and copies ran while one was open for 35% of the time, Pallas kernels for 0%

commit v1 on v0

v1 whole, which is shorter than its diff:
```python
import functools
import math

import jax
import jax.numpy as jnp
import ml_dtypes
import numpy as np
from jax import lax
from jax.experimental import pallas as pl
from jax.experimental.pallas import tpu as pltpu
from jax.sharding import PartitionSpec as P

HARM = 9
NC = 19
ND = 512
NIF = 128
NT = 128
PTS = 128
NX, NZ, NY = 4, 8, 4
NDEV = 128
TILES = 152
ROWS = 128
STIFF = 0.3
FRICTION = 0.6
MESH = pl.DeviceIdType.MESH
BF = jnp.bfloat16
F32 = jnp.float32


def high_low(table):
    high = table.astype(ml_dtypes.bfloat16)
    low = (table - high.astype(np.float64)).astype(ml_dtypes.bfloat16)
    return high, low


def fourier_tables():
    comp = np.arange(NC)
    order = np.where(comp <= HARM, comp, comp - HARM).astype(np.float64)
    phase = order[:, None] * (np.arange(NT) * (2.0 * math.pi / NT))[None, :]
    sine = (comp > HARM)[:, None]
    slope = np.where(sine, order[:, None] * np.cos(phase), -order[:, None] * np.sin(phase))
    shape = np.where(sine, np.sin(phase), np.cos(phase))
    weight = np.where(comp == 0, 1.0 / NT, 2.0 / NT)
    eye = np.eye(8)
    s_hi, s_lo = high_low(slope[1:].T)
    p_hi, p_lo = high_low(shape * weight[:, None])
    spread = lambda t: np.kron(t.astype(np.float64), eye).astype(ml_dtypes.bfloat16)
    slope_table = np.concatenate([spread(s_hi), spread(s_lo)], axis=1)
    proj_table = np.concatenate([spread(p_hi), spread(p_lo)], axis=0)
    return slope_table, proj_table


def dot(a, b):
    return jnp.dot(a, b, preferred_element_type=F32)


def main_kernel(
    src_ref, modal, stiff, mass, freq, rows_ref, tags, slope_t, proj_t,
    part_f, part_b, got, got_tags,
    packed, psend, rx, ysend, ry, zsend, rz, agz, agy, agx,
    pay, harm, force, resid, stm, scat,
    s_send, s_recv, t_send, t_recv, r_send, r_recv,
):
    sec = lax.axis_index("section")
    me = lax.axis_index("diam")
    other = 1 - sec
    x = me // (NZ * NY)
    z = lax.rem(me // NY, NZ)
    y = lax.rem(me, NY)

    def at(px, pz, py):
        return (px * NZ + pz) * NY + py

    def x_peer(k):
        return lax.rem(x + k, NX)

    def y_peer(k):
        return lax.rem(y + k, NY)

    def z_peer(k):
        return lax.rem(z + k, NZ)

    barrier = pltpu.get_barrier_semaphore()

    def hail(k, carry):
        pl.semaphore_signal(barrier, inc=1, device_id=(other, k), device_id_type=MESH)
        return carry

    lax.fori_loop(0, NDEV, hail, 0)
    for k in range(1, NX):
        pl.semaphore_signal(barrier, inc=1, device_id=(sec, at(x_peer(k), z, y)), device_id_type=MESH)
    for k in range(1, NY):
        pl.semaphore_signal(barrier, inc=1, device_id=(sec, at(x, z, y_peer(k))), device_id_type=MESH)
    for k in range(1, NZ):
        pl.semaphore_signal(barrier, inc=1, device_id=(sec, at(x, z_peer(k), y)), device_id_type=MESH)

    def pack(d, carry):
        packed[d, 0:32, :] = modal[src_ref[2 * d]]
        packed[d, 32:64, :] = modal[src_ref[2 * d + 1]]
        return carry

    lax.fori_loop(0, NDEV, pack, 0)
    pl.semaphore_wait(barrier, NDEV + NX + NY + NZ - 3)

    def send_tiles(first, count):
        def one(k, carry):
            px = lax.rem(x + k // (NZ * NY), NX)
            pz = lax.rem(z + lax.rem(k // NY, NZ), NZ)
            py = lax.rem(y + lax.rem(k, NY), NY)
            d = at(px, pz, py)
            pltpu.make_async_remote_copy(
                src_ref=tags.at[d], dst_ref=got_tags.at[me], send_sem=t_send, recv_sem=t_recv,
                device_id=(other, d), device_id_type=MESH,
            ).start()
            pltpu.make_async_remote_copy(
                src_ref=packed.at[d], dst_ref=got.at[me], send_sem=s_send, recv_sem=s_recv,
                device_id=(other, d), device_id_type=MESH,
            ).start()
            return carry

        lax.fori_loop(first, first + count, one, 0)

    send_tiles(0, 32)

    pre_row = rows_ref[0:1, :]
    eval_row = rows_ref[1:2, :]
    dof_row = rows_ref[2:3, :]
    dof_col = jnp.transpose(jnp.broadcast_to(dof_row, (ROWS, ROWS)))
    lane512 = lax.broadcasted_iota(jnp.int32, (ROWS, ND), 1).astype(F32)
    sub512 = lax.broadcasted_iota(jnp.int32, (ND, ROWS), 0).astype(F32)
    picks = []
    for g in range(2):
        halves = []
        for a in range(2):
            here = dof_col[:, 0:1] * 2.0 + (a - g * ND)
            halves.append(jnp.where(lane512 == here, 1.0, 0.0).astype(BF))
            there = dof_row * 2.0 + (a - g * ND)
            scat[g, :, a * ROWS:(a + 1) * ROWS] = jnp.where(sub512 == there, 1.0, 0.0).astype(BF)
        picks.append(jnp.concatenate(halves, axis=0))
    sub128 = lax.broadcasted_iota(jnp.int32, (ROWS, ROWS), 0).astype(F32)
    weights32 = jnp.where(sub128 == eval_row, pre_row, 0.0)
    weights = weights32.astype(BF)
    load = jnp.broadcast_to(jnp.sum(weights32, axis=1, keepdims=True), (NDEV, PTS))
    load_hi = load.astype(BF)
    psend[:, :, 38] = load_hi.reshape(NX, 2, 16, PTS)
    psend[:, :, 39] = (load - load_hi.astype(F32)).astype(BF).reshape(NX, 2, 16, PTS)

    def comps(g, c, n):
        tiles = [modal[pl.ds(((g * NC) + c + i) * 16, 16)].reshape(ND, PTS) for i in range(n)]
        return tiles[0] if n == 1 else jnp.concatenate(tiles, axis=1)

    def gather(c, n):
        got_rows = dot(picks[0], comps(0, c, n)) + dot(picks[1], comps(1, c, n))
        narrow = got_rows.astype(BF)
        for i in range(n):
            pay[c + i] = got_rows[:, i * PTS:(i + 1) * PTS]
        for a in range(2):
            summed = dot(weights, narrow[a * ROWS:(a + 1) * ROWS]).astype(BF)
            for i in range(n):
                psend[:, :, (c + i) * 2 + a] = summed[:, i * PTS:(i + 1) * PTS].reshape(NX, 2, 16, PTS)

    def gather_pair(i, carry):
        gather(2 * i, 2)
        return carry

    lax.fori_loop(0, 9, gather_pair, 0)
    gather(18, 1)

    def push(src, dst, step, device):
        pltpu.make_async_remote_copy(
            src_ref=src, dst_ref=dst, send_sem=r_send.at[step], recv_sem=r_recv.at[step],
            device_id=device, device_id_type=MESH,
        ).start()

    def arrived(ref, step):
        pltpu.make_async_copy(ref, ref, r_recv.at[step]).wait()

    def left(ref, step):
        pltpu.make_async_copy(ref, ref, r_send.at[step]).wait()

    for k in range(1, NX):
        push(psend.at[x_peer(k)], rx.at[x], 0, (sec, at(x_peer(k), z, y)))
    send_tiles(32, 32)

    for g in range(2):
        stm[g, 0:ND] = jnp.transpose(stiff[g])
        stm[g, ND:2 * ND] = jnp.transpose(mass[g])

    soft = 0.01 / (freq[...] * freq[...])

    def contact(b, carry):
        low = pl.multiple_of(b * 8, 8)
        sides = []
        for a in range(2):
            lines = [pay[c, pl.ds(a * ROWS + low, 8), :] for c in range(1, NC)]
            sides.append(jnp.concatenate(lines, axis=0))
        values = jnp.concatenate(sides, axis=1).astype(BF)
        speed = dot(slope_t[...], jnp.concatenate([values, values], axis=0))
        one, two = speed[:, 0:PTS], speed[:, PTS:2 * PTS]
        inverse = lax.rsqrt(one * one + two * two + soft)
        slide = jnp.concatenate([(one * inverse).astype(BF), (two * inverse).astype(BF)], axis=1)
        both = dot(proj_t[...], slide)
        total = both[0:8 * NC] + both[8 * NC:16 * NC]
        for c in range(NC):
            for a in range(2):
                harm[c, pl.ds(a * ROWS + low, 8), :] = total[8 * c:8 * c + 8, a * PTS:(a + 1) * PTS]
        return carry

    lax.fori_loop(0, 8, contact, 0)

    arrived(rx.at[0:3], 0)
    whole = psend[x].astype(F32)
    for k in range(1, NX):
        whole = whole + rx[x_peer(k)].astype(F32)
    total = whole[:, 38] + whole[:, 39]
    total_hi = total.astype(BF)
    for g in range(2):
        for part in range(2):
            ysend[2 * g + part] = whole[g, 20 * part:20 * part + 20].astype(BF)
        ysend[2 * g + 1, 18] = total_hi[g]
        ysend[2 * g + 1, 19] = (total[g] - total_hi[g].astype(F32)).astype(BF)
    for k in range(1, NY):
        push(ysend.at[y_peer(k)], ry.at[y], 1, (sec, at(x, z, y_peer(k))))
    send_tiles(64, 32)
    lax.fori_loop(8, 16, contact, 0)

    arrived(ry.at[0:3], 1)
    whole = ysend[y].astype(F32)
    for k in range(1, NY):
        whole = whole + ry[y_peer(k)].astype(F32)
    total = whole[18] + whole[19]
    total_hi = total.astype(BF)
    odd = lax.rem(y, 2) == 1
    zsend[0:18] = whole[0:18].astype(BF)
    zsend[18] = jnp.where(odd, total, whole[18]).astype(BF)
    zsend[19] = jnp.where(odd, total - total_hi.astype(F32), whole[19]).astype(BF)
    zsend[20:24] = jnp.zeros((4, 16, PTS), BF)
    for k in range(1, NZ):
        push(zsend.at[pl.ds(3 * z_peer(k), 3)], rz.at[z], 2, (sec, at(x, z_peer(k), y)))
    send_tiles(96, 32)

    def balance(g, c, n):
        both = dot(stm[g], comps(g, c, n))
        for i in range(n):
            h = jnp.where(c + i <= HARM, c + i, c + i - HARM)
            scaled = jnp.asarray(h, jnp.int32).astype(F32) * freq[...]
            lanes = slice(i * PTS, (i + 1) * PTS)
            resid[g * NC + c + i] = both[0:ND, lanes] - (scaled * scaled) * both[ND:2 * ND, lanes]

    def balance_pair(g, i, carry):
        balance(g, 2 * i, 2)
        return carry

    lax.fori_loop(0, 9, functools.partial(balance_pair, 0), 0)
    balance(0, 18, 1)

    arrived(rz.at[0:7], 2)
    whole = zsend[pl.ds(3 * z, 3)].astype(F32)
    for k in range(1, NZ):
        whole = whole + rz[z_peer(k)].astype(F32)
    total = whole[0] + whole[1]
    total_hi = total.astype(BF)
    loads = jnp.logical_and(odd, z == 6)
    agz[3 * z] = jnp.where(loads, total, whole[0]).astype(BF)
    agz[3 * z + 1] = jnp.where(loads, total - total_hi.astype(F32), whole[1]).astype(BF)
    agz[3 * z + 2] = whole[2].astype(BF)
    for k in range(1, NZ):
        mine = agz.at[pl.ds(3 * z, 3)]
        push(mine, mine, 3, (sec, at(x, z_peer(k), y)))
    lax.fori_loop(0, 4, functools.partial(balance_pair, 1), 0)
    arrived(agz.at[0:21], 3)
    agy[pl.ds(20 * y, 20)] = agz[0:20]
    for k in range(1, NY):
        push(agz.at[0:20], agy.at[pl.ds(20 * y, 20)], 4, (sec, at(x, z, y_peer(k))))
    lax.fori_loop(4, 6, functools.partial(balance_pair, 1), 0)
    arrived(agy.at[0:60], 4)
    agx[x] = agy[...].reshape(2, 40, 16, PTS)
    for k in range(1, NX):
        push(agx.at[x], agx.at[x], 5, (sec, at(x_peer(k), z, y)))
    lax.fori_loop(6, 9, functools.partial(balance_pair, 1), 0)
    balance(1, 18, 1)
    arrived(agx.at[0:3], 5)

    lane128 = lax.broadcasted_iota(jnp.int32, (ROWS, ROWS), 1).astype(F32)
    eval_col = jnp.transpose(jnp.broadcast_to(eval_row, (ROWS, ROWS)))
    pre_col = jnp.transpose(jnp.broadcast_to(pre_row, (ROWS, ROWS)))
    choose = jnp.where(lane128 == eval_col, 1.0, 0.0).astype(BF)

    def joints(k):
        return agx[:, :, k].reshape(NDEV, PTS)

    loaded = dot(choose, jnp.concatenate([joints(38), joints(39)], axis=1))
    per_load = 1.0 / (loaded[:, 0:PTS] + loaded[:, PTS:2 * PTS])
    pressed = pre_col * (FRICTION * ROWS) * per_load

    def forces(c, carry):
        mean = dot(choose, jnp.concatenate([joints(2 * c), joints(2 * c + 1)], axis=1))
        for a in range(2):
            rows = slice(a * ROWS, (a + 1) * ROWS)
            away = pay[c, rows, :] - mean[:, a * PTS:(a + 1) * PTS] * per_load
            force[c, rows, :] = (STIFF * away + pressed * harm[c, rows, :]).astype(BF)
        return carry

    lax.fori_loop(0, NC, forces, 0)

    def finish(g, c, n):
        lines = [force[c + i] for i in range(n)]
        added = dot(scat[g], lines[0] if n == 1 else jnp.concatenate(lines, axis=1))
        for i in range(n):
            item = g * NC + c + i
            value = resid[item] + added[:, i * PTS:(i + 1) * PTS]
            part_f[item] = value[0:NIF]
            part_b[item] = value[NIF:ND].astype(BF)

    def finish_pair(g, i, carry):
        finish(g, 2 * i, 2)
        return carry

    for g in range(2):
        lax.fori_loop(0, 9, functools.partial(finish_pair, g), 0)
        finish(g, 18, 1)

    left(rx.at[0:3], 0)
    left(ry.at[0:3], 1)
    left(rz.at[0:7], 2)
    left(rz.at[0:7], 3)
    left(agy.at[0:60], 4)
    left(agx.at[0:3], 5)
    pltpu.make_async_copy(packed, packed, s_send).wait()
    pltpu.make_async_copy(tags, tags, t_send).wait()
    pltpu.make_async_copy(got_tags, got_tags, t_recv).wait()
    pltpu.make_async_copy(got, got, s_recv).wait()


def last_kernel(tag_ref, got, part_f, part_b, link, out, glued):
    step = pl.program_id(0)

    @pl.when(step == 0)
    def _():
        glued[...] = jnp.zeros_like(glued)

        def add(d, carry):
            for s in range(2):
                slot = tag_ref[2 * d + s]
                glued[slot] = glued[slot] + got[d, 32 * s:32 * s + 32, :].astype(F32)
            return carry

        lax.fori_loop(0, NDEV, add, 0)

    for i in range(2):
        item = step * 2 + i
        tiles = glued[pl.ds(item * 4, 4)].reshape(NIF, PTS).astype(BF)
        out[i, 0:NIF, :] = (part_f[i] + dot(link[item // NC], tiles)).astype(BF)
        out[i, NIF:ND, :] = part_b[i]


def body(modal, stiffness, mass, freq, coupling, route, target, contact_dof, evaluator, preload):
    tiles = modal.reshape(2 * NC * 16, 32, PTS)
    place = jnp.arange(TILES, dtype=jnp.int32)
    key = (place * 256 + target[0])[None, :]
    named = route[0, :, 0][None, :] == jnp.arange(NDEV, dtype=jnp.int32)[:, None]
    first = jnp.min(jnp.where(named, key, 1 << 20), axis=1)
    final = jnp.max(jnp.where(named, key, -1), axis=1)
    pair = jnp.stack([jnp.where(first < (1 << 20), first, TILES),
                      jnp.where((final >= 0) & (final != first), final, TILES)], axis=1)
    spot = pair // 256
    src = ((spot // 4) * 16 + spot % 4).reshape(2 * NDEV)
    tags = jnp.broadcast_to((pair % 256)[:, :, None], (NDEV, 2, 64)).reshape(NDEV, 1, 128)
    rows = jnp.concatenate([
        preload.astype(F32), evaluator[:, :, 0].astype(F32), contact_dof.astype(F32),
        jnp.zeros((5, ROWS), F32)], axis=0)
    same = jnp.eye(4, dtype=jnp.bool_)[None, :, None, :, None]
    link = jnp.where(same, jnp.swapaxes(coupling[0], 2, 3)[:, :, :, None, :], 0).astype(BF)
    link = link.reshape(2, NIF, NIF)
    slope_table, proj_table = fourier_tables()

    vmem = pl.BlockSpec(memory_space=pltpu.VMEM)
    anywhere = pl.BlockSpec(memory_space=pl.ANY)
    dma = pltpu.SemaphoreType.DMA
    part_f, part_b, got, got_tags = pl.pallas_call(
        main_kernel,
        out_shape=(
            jax.ShapeDtypeStruct((2 * NC, NIF, PTS), F32),
            jax.ShapeDtypeStruct((2 * NC, ND - NIF, PTS), BF),
            jax.ShapeDtypeStruct((NDEV, 64, PTS), BF),
            jax.ShapeDtypeStruct((NDEV, 1, 128), jnp.int32),
        ),
        in_specs=[pl.BlockSpec(memory_space=pltpu.SMEM)] + [vmem] * 8,
        out_specs=(vmem, vmem, anywhere, anywhere),
        scratch_shapes=[
            pltpu.VMEM((NDEV, 64, PTS), BF),
            pltpu.VMEM((NX, 2, 40, 16, PTS), BF),
            pltpu.VMEM((NX, 2, 40, 16, PTS), BF),
            pltpu.VMEM((NY, 20, 16, PTS), BF),
            pltpu.VMEM((NY, 20, 16, PTS), BF),
            pltpu.VMEM((24, 16, PTS), BF),
            pltpu.VMEM((NZ, 3, 16, PTS), BF),
            pltpu.VMEM((24, 16, PTS), BF),
            pltpu.VMEM((80, 16, PTS), BF),
            pltpu.VMEM((NX, 2, 40, 16, PTS), BF),
            pltpu.VMEM((NC, 2 * ROWS, PTS), F32),
            pltpu.VMEM((NC, 2 * ROWS, PTS), F32),
            pltpu.VMEM((NC, 2 * ROWS, PTS), BF),
            pltpu.VMEM((2 * NC, ND, PTS), F32),
            pltpu.VMEM((2, 2 * ND, ND), BF),
            pltpu.VMEM((2, ND, 2 * ROWS), BF),
            dma, dma, dma, dma, dma((6,)), dma((6,)),
        ],
        compiler_params=pltpu.CompilerParams(
            collective_id=1, has_side_effects=True, vmem_limit_bytes=58 << 20
        ),
    )(src, tiles, stiffness[0], mass[0], freq.reshape(1, PTS), rows, tags,
      jnp.asarray(slope_table), jnp.asarray(proj_table))

    tag_list = jnp.concatenate([got_tags[:, :, 0], got_tags[:, :, 64]], axis=1).reshape(2 * NDEV)
    out = pl.pallas_call(
        last_kernel,
        grid=(NC,),
        out_shape=jax.ShapeDtypeStruct((2 * NC, ND, PTS), BF),
        in_specs=[
            pl.BlockSpec(memory_space=pltpu.SMEM),
            pl.BlockSpec((NDEV, 64, PTS), lambda i: (0, 0, 0)),
            pl.BlockSpec((2, NIF, PTS), lambda i: (i, 0, 0)),
            pl.BlockSpec((2, ND - NIF, PTS), lambda i: (i, 0, 0)),
            pl.BlockSpec((2, NIF, NIF), lambda i: (0, 0, 0)),
        ],
        out_specs=pl.BlockSpec((2, ND, PTS), lambda i: (i, 0, 0)),
        scratch_shapes=[pltpu.VMEM((TILES + 1, 32, PTS), F32)],
        compiler_params=pltpu.CompilerParams(vmem_limit_bytes=32 << 20),
    )(tag_list, got, part_f, part_b, link)
    return out.reshape(1, 2, NC, ND, PTS)


def solution(mesh):
    placed = (
        P("section", "diam", None, None, None),
        P("section", "diam", None, None),
        P("section", "diam", None, None),
        P(),
        P("section", "diam", None, None, None),
        P("section", "diam", None),
        P("section", "diam"),
        P("section", "diam"),
        P("section", "diam", None),
        P("section", "diam"),
    )
    return jax.shard_map(
        body,
        mesh=mesh,
        in_specs=placed,
        out_specs=P("section", "diam", None, None, None),
        check_vma=False,
    )
```

time: 595 us -> 141 us (0.24); the launches traced: 586 us -> 141 us
  other arithmetic: 271 us -> 4.71 us
  Pallas kernels: 0 us -> 122 us
  local copies, waits for them, and re-layouts: 108 us -> 13.8 us
  matrix products: 83.4 us -> 0 us
  starting transfers between devices: 69.8 us -> 0 us
  waiting for transfers between devices: 53.9 us -> 0 us
    unnamed x5 -> x0, other arithmetic: 235 us -> none
    pallas_call x0 -> x2, Pallas kernels: none -> 122 us  [the longest x1 111 us: body(): pl.pallas_call(main_kernel, out_shape=(jax.ShapeDtypeStruct((2 * NC, NIF,...]
    dot_general x13 -> x0, matrix products: 83.4 us -> none  [the longest x4 40.4 us: joint_forces(): jnp.einsum('sjpt,tc->scjp', sliding, projection, precision=lax.Precision....]
    all_to_all x5 -> x0, starting transfers between devices: 69 us -> none  [the longest x1 16.2 us: body(): lax.all_to_all(send_load.reshape(width, depth_rows), 'diam', split_axis=0...]
    all_to_all x5 -> x0, waiting for transfers between devices: 53.2 us -> none  [the longest x1 36.4 us: body(): lax.all_to_all(computed.reshape(width, depth_rows, comp_total, 2, point_t...]
    gather x2 -> x0, local copies, waits for them, and re-layouts: 42.1 us -> none  [the longest x1 36.3 us: body(): by_pairs[block_index[:, None], jnp.arange(comp_total)[None, :], dof_pair[...]
    scatter x4 -> x0, local copies, waits for them, and re-layouts: 33.3 us -> none  [the longest x1 19 us: body(): packed = jnp.zeros((width * depth_tiles, NIFP, point_total), jnp.bfloat16...]
    div x6 -> x0, other arithmetic: 9.8 us -> none  [the longest x4 6.16 us: joint_forces(): FRICTION * pressure[:, None, None, None] * velocity / slip_speed[:, None]]
  transfers between devices with their start and end apart: 7 -> 0, of which waited for: 3 -> 0; matrix products, arithmetic and copies ran while one was open for 35% -> 0% of each run, Pallas kernels for 0% -> 0%
where the time goes in v1:
time: 141 us
  Pallas kernels  122 us (87%)
  local copies, waits for them, and re-layouts  13.8 us (10%)
  other arithmetic  4.71 us (3%)
    pallas_call x1, Pallas kernels, body(): pl.pallas_call(main_kernel, out_shape=(jax.ShapeDtypeStruct((2 * NC, NIF,...  111 us
    pallas_call x1, Pallas kernels, body(): pl.pallas_call(last_kernel, grid=(NC,), out_shape=jax.ShapeDtypeStruct((2...  10.9 us
    slice x1, local copies, waits for them, and re-layouts, body(): got_tags[:, :, 0]  5.73 us
    unnamed x6, local copies, waits for them, and re-layouts  5.35 us

profile of v1, /device:TPU:4, one launch (start us, length us, event | category | flops | bytes accessed | tf_op | source)
XLA Modules:
  0.0 140.7 jit_solution(12104425991581475463)
XLA Ops:
  0.0 0.7 convert_element_type.25
  0.7 0.7 convert_bitcast_fusion
  1.3 0.7 convert_element_type.22
  2.0 0.1 pad.5.clone
  2.1 0.7 multiply_add_fusion
  2.7 0.8 select_reduce_fusion.1
  3.6 0.7 maximum_maximum_fusion.rows_ref
  4.2 0.7 copy.20.tags
  5.0 0.1 broadcast_in_dim.71
  5.1 0.1 broadcast_in_dim.72
  5.2 0.1 copy.19
  5.3 0.1 stack.8
  5.5 0.5 fusion.src_ref
  6.0 0.9 copy.22
  7.0 0.1 broadcast_in_dim.74
  7.1 0.2 broadcast_in_dim.75
  7.2 111.2 %shard_map.118 = (f32[38,128,128]{2,1,0:T(8,128)}, bf16[38,384,128]{2,1,0:T(8,128)(2,1)}, bf16[128,64,128]{2,1,0:T(8,128)(2,1)}, s32[128,1,128]{2,1,0:T(1,128)}) custom-call(s32[256]{0:T(256)} %fusion.src_ref, bf16[608,32,128]{2,1,0:T(8,128)(2,1)} %bitcast.20, bf16[2,512,512]{2,1,0:T(8,128)(2,1)} %bitcast.21, bf16[2,512,512]{2,1,0:T(8,128)(2,1)} %bitcast.22, ...), custom_call_target="tpu_custom_call" | custom-call | tf_op jit(solution)/shard_map/pallas_call | solution.py:380
  118.5 5.7 %slice_reduce_fusion.1 = (s32[128]{0:T(128)S(1)}, s32[128]{0:T(128)S(1)}) fusion(s32[128,1,128]{2,1,0:T(1,128)} %get-tuple-element.9), kind=kLoop, calls=%fused_computation.4 | loop fusion | bytes 2048 | tf_op jit(solution)/shard_map/slice | solution.py:415
  124.2 0.1 copy.21
  124.3 0.1 reshape.131.tag_ref
  124.5 0.0 copy-start
  124.5 2.1 %copy-done = bf16[38,384,128]{2,1,0:T(8,128)(2,1)S(1)} copy-done((bf16[38,384,128]{2,1,0:T(8,128)(2,1)S(1)}, bf16[38,384,128]{2,1,0:T(8,128)(2,1)}, u32[]{:S(2)}) %copy-start) | copy-done | bytes 3735576
  126.6 0.0 copy-start.1
  126.6 1.7 %copy-done.1 = f32[38,128,128]{2,1,0:T(8,128)S(1)} copy-done((f32[38,128,128]{2,1,0:T(8,128)S(1)}, f32[38,128,128]{2,1,0:T(8,128)}, u32[]{:S(2)}) %copy-start.1) | copy-done | bytes 2490392
  128.3 0.0 copy-start.2
  128.3 1.6 %copy-done.2 = bf16[128,64,128]{2,1,0:T(8,128)(2,1)S(1)} copy-done((bf16[128,64,128]{2,1,0:T(8,128)(2,1)S(1)}, bf16[128,64,128]{2,1,0:T(8,128)(2,1)}, u32[]{:S(2)}) %copy-start.2) | copy-done | bytes 2097176
  129.9 10.9 %shard_map.119 = bf16[38,512,128]{2,1,0:T(8,128)(2,1)} custom-call(s32[256]{0:T(256)S(1)} %reshape.131.tag_ref, bf16[128,64,128]{2,1,0:T(8,128)(2,1)S(1)} %copy-done.2, f32[38,128,128]{2,1,0:T(8,128)S(1)} %copy-done.1, bf16[38,384,128]{2,1,0:T(8,128)(2,1)S(1)} %copy-done, bf16[2,128,128]{2,1,0:T(8,128)(2,1)S(1)} %broadcast_select_fusion.link), custom_call_target="tpu_custom_call" | custom-call | tf_op jit(solution)/shard_map/pallas_call | solution.py:416
  (7 shorter events, 0.1 us)
Async XLA Ops:
  124.5 2.1 %copy-start = (bf16[38,384,128]{2,1,0:T(8,128)(2,1)S(1)}, bf16[38,384,128]{2,1,0:T(8,128)(2,1)}, u32[]{:S(2)}) copy-start(bf16[38,384,128]{2,1,0:T(8,128)(2,1)} %get-tuple-element.12.part_b) | copy-start | bytes 11206660
  126.6 1.7 %copy-start.1 = (f32[38,128,128]{2,1,0:T(8,128)S(1)}, f32[38,128,128]{2,1,0:T(8,128)}, u32[]{:S(2)}) copy-start(f32[38,128,128]{2,1,0:T(8,128)} %get-tuple-element.11.part_f) | copy-start | bytes 7471108
  128.3 1.6 %copy-start.2 = (bf16[128,64,128]{2,1,0:T(8,128)(2,1)S(1)}, bf16[128,64,128]{2,1,0:T(8,128)(2,1)}, u32[]{:S(2)}) copy-start(bf16[128,64,128]{2,1,0:T(8,128)(2,1)} %get-tuple-element.10.got) | copy-start | bytes 6291460

commit v2 on v1

v2 whole, which is shorter than its diff:
```python
import functools
import math

import jax
import jax.numpy as jnp
import ml_dtypes
import numpy as np
from jax import lax
from jax.experimental import pallas as pl
from jax.experimental.pallas import tpu as pltpu
from jax.sharding import PartitionSpec as P

HARM = 9
NC = 19
ND = 512
NIF = 128
NT = 128
PTS = 128
NX, NZ, NY = 4, 8, 4
NDEV = 128
TILES = 152
ROWS = 128
STIFF = 0.3
FRICTION = 0.6
MESH = pl.DeviceIdType.MESH
BF = jnp.bfloat16
F32 = jnp.float32


def high_low(table):
    high = table.astype(ml_dtypes.bfloat16)
    low = (table - high.astype(np.float64)).astype(ml_dtypes.bfloat16)
    return high, low


def fourier_tables():
    comp = np.arange(NC)
    order = np.where(comp <= HARM, comp, comp - HARM).astype(np.float64)
    phase = order[:, None] * (np.arange(NT) * (2.0 * math.pi / NT))[None, :]
    sine = (comp > HARM)[:, None]
    slope = np.where(sine, order[:, None] * np.cos(phase), -order[:, None] * np.sin(phase))
    shape = np.where(sine, np.sin(phase), np.cos(phase))
    weight = np.where(comp == 0, 1.0 / NT, 2.0 / NT)
    eye = np.eye(8)
    s_hi, s_lo = high_low(slope[1:].T)
    p_hi, p_lo = high_low(shape * weight[:, None])
    spread = lambda t: np.kron(t.astype(np.float64), eye).astype(ml_dtypes.bfloat16)
    slope_table = np.concatenate([spread(s_hi), spread(s_lo)], axis=1)
    proj_table = np.concatenate([spread(p_hi), spread(p_lo)], axis=0)
    return slope_table, proj_table


def dot(a, b):
    return jnp.dot(a, b, preferred_element_type=F32)


def main_kernel(
    modal_h, stiff_h, mass_h, freq, pre_ref, eval_ref, dof_ref, route_ref, target_ref,
    slope_t, proj_t,
    part_f, part_b, got, got_tags,
    edge, inner, stiff, mass, source, source_s, tags, packed,
    psend, rx, ysend, ry, zsend, rz, agz, agy, agx,
    pay, harm, force, resid, stm, scat, near, far,
    l_sem, s_send, s_recv, t_send, t_recv, r_send, r_recv,
):
    sec = lax.axis_index("section")
    me = lax.axis_index("diam")
    other = 1 - sec
    x = me // (NZ * NY)
    z = lax.rem(me // NY, NZ)
    y = lax.rem(me, NY)

    def at(px, pz, py):
        return (px * NZ + pz) * NY + py

    def x_peer(k):
        return lax.rem(x + k, NX)

    def y_peer(k):
        return lax.rem(y + k, NY)

    def z_peer(k):
        return lax.rem(z + k, NZ)

    loads = [
        pltpu.make_async_copy(modal_h.at[:, 0:4], edge, l_sem.at[0]),
        pltpu.make_async_copy(modal_h.at[:, 4:16], inner, l_sem.at[1]),
        pltpu.make_async_copy(stiff_h, stiff, l_sem.at[2]),
        pltpu.make_async_copy(mass_h, mass, l_sem.at[3]),
    ]
    for load in loads:
        load.start()

    barrier = pltpu.get_barrier_semaphore()

    def hail(k, carry):
        pl.semaphore_signal(barrier, inc=1, device_id=(other, k), device_id_type=MESH)
        return carry

    lax.fori_loop(0, NDEV, hail, 0)
    for k in range(1, NX):
        pl.semaphore_signal(barrier, inc=1, device_id=(sec, at(x_peer(k), z, y)), device_id_type=MESH)
    for k in range(1, NY):
        pl.semaphore_signal(barrier, inc=1, device_id=(sec, at(x, z, y_peer(k))), device_id_type=MESH)
    for k in range(1, NZ):
        pl.semaphore_signal(barrier, inc=1, device_id=(sec, at(x, z_peer(k), y)), device_id_type=MESH)

    spot = lax.broadcasted_iota(jnp.int32, (NDEV, TILES), 1)
    named = route_ref[...] == lax.broadcasted_iota(jnp.int32, (NDEV, TILES), 0)
    key = (spot * 256 + target_ref[...])
    first = jnp.min(jnp.where(named, key, 1 << 20), axis=1, keepdims=True)
    final = jnp.max(jnp.where(named, key, -1), axis=1, keepdims=True)
    none = jnp.full_like(first, TILES)
    one_key = jnp.where(first < (1 << 20), first, none)
    two_key = jnp.where((final >= 0) & (final != first), final, none)
    lane = lax.broadcasted_iota(jnp.int32, (NDEV, 128), 1)
    keys = jnp.where(lane < 64, one_key, two_key)
    source[...] = jnp.right_shift(keys, 8)
    tags[...] = jnp.bitwise_and(keys, 255).reshape(NDEV, 1, 128)
    listing = pltpu.make_async_copy(source, source_s, l_sem.at[4])
    listing.start()
    listing.wait()
    loads[0].wait()

    def tile(t):
        return edge[jnp.right_shift(t, 2), jnp.bitwise_and(t, 3)]

    def pack(d, carry):
        packed[d, 0:32, :] = tile(source_s[d, 0])
        packed[d, 32:64, :] = tile(source_s[d, 64])
        return carry

    lax.fori_loop(0, NDEV, pack, 0)
    pl.semaphore_wait(barrier, NDEV + NX + NY + NZ - 3)

    def send_one(k):
        px = lax.rem(x + k // (NZ * NY), NX)
        pz = lax.rem(z + lax.rem(k, NZ), NZ)
        py = lax.rem(y + lax.rem(k // NZ, NY), NY)
        d = at(px, pz, py)
        pltpu.make_async_remote_copy(
            src_ref=tags.at[d], dst_ref=got_tags.at[me], send_sem=t_send, recv_sem=t_recv,
            device_id=(other, d), device_id_type=MESH,
        ).start()
        pltpu.make_async_remote_copy(
            src_ref=packed.at[d], dst_ref=got.at[me], send_sem=s_send, recv_sem=s_recv,
            device_id=(other, d), device_id_type=MESH,
        ).start()

    def send_tiles(first, count):
        def one(k, carry):
            send_one(k)
            return carry

        lax.fori_loop(first, first + count, one, 0)

    send_tiles(0, 24)

    pre_row = pre_ref[...].astype(F32)
    eval_row = eval_ref[...].astype(F32)
    dof_row = dof_ref[...].astype(F32)
    dof_col = jnp.transpose(jnp.broadcast_to(dof_row, (ROWS, ROWS)))
    lane512 = lax.broadcasted_iota(jnp.int32, (ROWS, ND), 1).astype(F32)
    sub512 = lax.broadcasted_iota(jnp.int32, (ND, ROWS), 0).astype(F32)
    picks = []
    for g in range(2):
        halves = []
        for a in range(2):
            here = dof_col[:, 0:1] * 2.0 + (a - g * ND)
            halves.append(jnp.where(lane512 == here, 1.0, 0.0).astype(BF))
            there = dof_row * 2.0 + (a - g * ND)
            scat[g, :, a * ROWS:(a + 1) * ROWS] = jnp.where(sub512 == there, 1.0, 0.0).astype(BF)
        picks.append(jnp.concatenate(halves, axis=0))
    sub128 = lax.broadcasted_iota(jnp.int32, (ROWS, ROWS), 0).astype(F32)
    weights32 = jnp.where(sub128 == eval_row, pre_row, 0.0)
    weights = weights32.astype(BF)
    load = jnp.broadcast_to(jnp.sum(weights32, axis=1, keepdims=True), (NDEV, PTS))
    load_hi = load.astype(BF)
    psend[1, :, :, 18] = load_hi.reshape(4, 2, 16, PTS)
    psend[1, :, :, 19] = (load - load_hi.astype(F32)).astype(BF).reshape(4, 2, 16, PTS)
    loads[1].wait()

    def comps(g, c, n):
        tiles = []
        for i in range(n):
            item = g * NC + c + i
            parts = [edge[item].reshape(NIF, PTS), inner[item].reshape(ND - NIF, PTS)]
            tiles.append(jnp.concatenate(parts, axis=0))
        return tiles[0] if n == 1 else jnp.concatenate(tiles, axis=1)

    def gather(c, n, half):
        got_rows = dot(picks[0], comps(0, c, n)) + dot(picks[1], comps(1, c, n))
        narrow = got_rows.astype(BF)
        for i in range(n):
            pay[c + i] = got_rows[:, i * PTS:(i + 1) * PTS]
        for a in range(2):
            summed = dot(weights, narrow[a * ROWS:(a + 1) * ROWS]).astype(BF)
            for i in range(n):
                part = summed[:, i * PTS:(i + 1) * PTS].reshape(4, 2, 16, PTS)
                psend[half, :, :, (c + i) * 2 + a - 20 * half] = part

    def gather_pair(half, i, carry):
        send_one(24 + 2 * i)
        gather(2 * i, 2, half)
        send_one(25 + 2 * i)
        return carry

    lax.fori_loop(0, 5, functools.partial(gather_pair, 0), 0)
    lax.fori_loop(5, 9, functools.partial(gather_pair, 1), 0)
    gather(18, 1, 1)

    def push(src, dst, step, device):
        pltpu.make_async_remote_copy(
            src_ref=src, dst_ref=dst, send_sem=r_send.at[step], recv_sem=r_recv.at[step],
            device_id=device, device_id_type=MESH,
        ).start()

    def arrived(ref, step):
        pltpu.make_async_copy(ref, ref, r_recv.at[step]).wait()

    def left(ref, step):
        pltpu.make_async_copy(ref, ref, r_send.at[step]).wait()

    mine = ((x, y), (y, x))
    peers = ((x_peer, y_peer), (y_peer, x_peer))

    def device(half, turn, k):
        if half == turn:
            return sec, at(x_peer(k), z, y)
        return sec, at(x, z, y_peer(k))

    for k in range(1, 4):
        for half in range(2):
            push(psend.at[half, peers[half][0](k)], rx.at[half, mine[half][0]], 0, device(half, 0, k))
    loads[2].wait()
    loads[3].wait()
    for g in range(2):
        stm[g, 0:ND] = jnp.transpose(stiff[g])
        stm[g, ND:2 * ND] = jnp.transpose(mass[g])

    soft = 0.01 / (freq[...] * freq[...])

    def contact(b, carry):
        for i in range(3):
            send_one(42 + 3 * b + i)
        low = pl.multiple_of(b * 8, 8)
        sides = []
        for a in range(2):
            lines = [pay[c, pl.ds(a * ROWS + low, 8), :] for c in range(1, NC)]
            sides.append(jnp.concatenate(lines, axis=0))
        values = jnp.concatenate(sides, axis=1).astype(BF)
        speed = dot(slope_t[...], jnp.concatenate([values, values], axis=0))
        one, two = speed[:, 0:PTS], speed[:, PTS:2 * PTS]
        inverse = lax.rsqrt(one * one + two * two + soft)
        slide = jnp.concatenate([(one * inverse).astype(BF), (two * inverse).astype(BF)], axis=1)
        both = dot(proj_t[...], slide)
        total = both[0:8 * NC] + both[8 * NC:16 * NC]
        for c in range(NC):
            for a in range(2):
                harm[c, pl.ds(a * ROWS + low, 8), :] = total[8 * c:8 * c + 8, a * PTS:(a + 1) * PTS]
        return carry

    lax.fori_loop(0, 9, contact, 0)

    def split(total):
        high = total.astype(BF)
        return high, (total - high.astype(F32)).astype(BF)

    arrived(rx.at[:, 0:3], 0)
    for half in range(2):
        whole = psend[half, mine[half][0]].astype(F32)
        for k in range(1, 4):
            whole = whole + rx[half, peers[half][0](k)].astype(F32)
        for g in range(2):
            for part in range(2):
                ysend[half, 2 * g + part] = whole[g, 10 * part:10 * part + 10].astype(BF)
        if half == 1:
            high, low = split(whole[:, 18] + whole[:, 19])
            for g in range(2):
                ysend[1, 2 * g + 1, 8] = high[g]
                ysend[1, 2 * g + 1, 9] = low[g]
    for k in range(1, 4):
        for half in range(2):
            push(ysend.at[half, peers[half][1](k)], ry.at[half, mine[half][1]], 1, device(half, 1, k))
    lax.fori_loop(9, 13, contact, 0)

    odd = lax.rem(x, 2) == 1
    arrived(ry.at[:, 0:3], 1)
    zsend[5:8] = jnp.zeros((3, 4, 16, PTS), BF)
    for half in range(2):
        whole = ysend[half, mine[half][1]].astype(F32)
        for k in range(1, 4):
            whole = whole + ry[half, peers[half][1](k)].astype(F32)
        for part in range(5):
            zsend[part, 2 * half:2 * half + 2] = whole[2 * part:2 * part + 2].astype(BF)
        if half == 1:
            high, low = split(whole[8] + whole[9])
            zsend[4, 2] = jnp.where(odd, high.astype(F32), whole[8]).astype(BF)
            zsend[4, 3] = jnp.where(odd, low.astype(F32), whole[9]).astype(BF)
    for k in range(1, NZ):
        push(zsend.at[z_peer(k)], rz.at[z], 2, (sec, at(x, z_peer(k), y)))
    lax.fori_loop(13, 16, contact, 0)

    def balance(g, c, n):
        both = dot(stm[g], comps(g, c, n))
        for i in range(n):
            h = jnp.where(c + i <= HARM, c + i, c + i - HARM)
            scaled = jnp.asarray(h, jnp.int32).astype(F32) * freq[...]
            lanes = slice(i * PTS, (i + 1) * PTS)
            resid[g * NC + c + i] = both[0:ND, lanes] - (scaled * scaled) * both[ND:2 * ND, lanes]

    def balance_pair(g, i, carry):
        send_one(90 + 18 * g + 2 * i)
        balance(g, 2 * i, 2)
        send_one(91 + 18 * g + 2 * i)
        return carry

    arrived(rz.at[0:7], 2)
    whole = zsend[z].astype(F32)
    for k in range(1, NZ):
        whole = whole + rz[z_peer(k)].astype(F32)
    high, low = split(whole[2] + whole[3])
    here = jnp.logical_and(odd, z == 4)
    agz[z, 0:2] = whole[0:2].astype(BF)
    agz[z, 2] = jnp.where(here, high.astype(F32), whole[2]).astype(BF)
    agz[z, 3] = jnp.where(here, low.astype(F32), whole[3]).astype(BF)
    for k in range(1, NZ):
        push(agz.at[z], agz.at[z], 3, (sec, at(x, z_peer(k), y)))
    lax.fori_loop(0, 5, functools.partial(balance_pair, 0), 0)

    arrived(agz.at[0:7], 3)
    for half in range(2):
        agy[half, mine[half][1]] = agz[0:5, 2 * half:2 * half + 2].reshape(10, 16, PTS)
        for k in range(1, 4):
            slot = agy.at[half, mine[half][1]]
            push(slot, slot, 4, device(half, 1, k))
    lax.fori_loop(5, 9, functools.partial(balance_pair, 0), 0)
    balance(0, 18, 1)

    arrived(agy.at[:, 0:3], 4)
    for half in range(2):
        agx[half, mine[half][0]] = agy[half].reshape(2, 20, 16, PTS)
        for k in range(1, 4):
            slot = agx.at[half, mine[half][0]]
            push(slot, slot, 5, device(half, 0, k))
    lax.fori_loop(0, 9, functools.partial(balance_pair, 1), 0)
    balance(1, 18, 1)
    send_tiles(126, 2)
    arrived(agx.at[:, 0:3], 5)

    lane128 = lax.broadcasted_iota(jnp.int32, (ROWS, ROWS), 1).astype(F32)
    eval_col = jnp.transpose(jnp.broadcast_to(eval_row, (ROWS, ROWS)))
    pre_col = jnp.transpose(jnp.broadcast_to(pre_row, (ROWS, ROWS)))
    choose = jnp.where(lane128 == eval_col, 1.0, 0.0).astype(BF)

    def joints(half, k):
        return agx[half, :, :, k].reshape(NDEV, PTS)

    loaded = dot(choose, jnp.concatenate([joints(1, 18), joints(1, 19)], axis=1))
    per_load = 1.0 / (loaded[:, 0:PTS] + loaded[:, PTS:2 * PTS])
    pressed = pre_col * (FRICTION * ROWS) * per_load

    def forces(half, c, carry):
        k = 2 * c - 20 * half
        mean = dot(choose, jnp.concatenate([joints(half, k), joints(half, k + 1)], axis=1))
        for a in range(2):
            rows = slice(a * ROWS, (a + 1) * ROWS)
            away = pay[c, rows, :] - mean[:, a * PTS:(a + 1) * PTS] * per_load
            force[c, rows, :] = (STIFF * away + pressed * harm[c, rows, :]).astype(BF)
        return carry

    lax.fori_loop(0, 10, functools.partial(forces, 0), 0)
    lax.fori_loop(10, NC, functools.partial(forces, 1), 0)

    def finish(g, c, n):
        lines = [force[c + i] for i in range(n)]
        added = dot(scat[g], lines[0] if n == 1 else jnp.concatenate(lines, axis=1))
        for i in range(n):
            item = g * NC + c + i
            value = resid[item] + added[:, i * PTS:(i + 1) * PTS]
            near[item] = value[0:NIF]
            far[item] = value[NIF:ND].astype(BF)

    def finish_pair(g, i, carry):
        finish(g, 2 * i, 2)
        return carry

    stores = []
    for g in range(2):
        lax.fori_loop(0, 9, functools.partial(finish_pair, g), 0)
        finish(g, 18, 1)
        block = pl.ds(g * NC, NC)
        stores.append(pltpu.make_async_copy(far.at[block], part_b.at[block], l_sem.at[5 + g]))
        stores.append(pltpu.make_async_copy(near.at[block], part_f.at[block], l_sem.at[7 + g]))
        stores[-2].start()
        stores[-1].start()

    left(rx.at[:, 0:3], 0)
    left(ry.at[:, 0:3], 1)
    left(rz.at[0:7], 2)
    left(agz.at[0:7], 3)
    left(agy.at[:, 0:3], 4)
    left(agx.at[:, 0:3], 5)
    for store in stores:
        store.wait()
    pltpu.make_async_copy(packed, packed, s_send).wait()
    pltpu.make_async_copy(tags, tags, t_send).wait()
    pltpu.make_async_copy(got_tags, got_tags, t_recv).wait()
    pltpu.make_async_copy(got, got, s_recv).wait()


def last_kernel(
    got_h, tags_h, part_f, part_b, coupling, out_h,
    got, tags, near, out, glued, link, sems,
):
    tag_copy = pltpu.make_async_copy(tags_h, tags, sems.at[0])
    got_copy = pltpu.make_async_copy(got_h, got, sems.at[1])
    near_copy = pltpu.make_async_copy(part_f, near, sems.at[2])
    tag_copy.start()
    got_copy.start()
    near_copy.start()
    fars = []
    for g in range(2):
        block = pl.ds(g * NC, NC)
        fars.append(pltpu.make_async_copy(part_b.at[block], out.at[block, NIF:ND], sems.at[3 + g]))
        fars[g].start()
    glued[...] = jnp.zeros_like(glued)
    link[...] = jnp.zeros_like(link)
    for g in range(2):
        for q in range(4):
            span = slice(32 * q, 32 * q + 32)
            link[g, span, span] = jnp.transpose(coupling[g, q].astype(F32)).astype(BF)
    tag_copy.wait()
    got_copy.wait()

    def add(d, carry):
        for s in range(2):
            slot = tags[d, 0, 64 * s]
            glued[s, slot] = glued[s, slot] + got[d, 32 * s:32 * s + 32, :].astype(F32)
        return carry

    lax.fori_loop(0, NDEV, add, 0, unroll=4)
    near_copy.wait()

    def item(g, c):
        span = pl.ds((g * NC + c) * 4, 4)
        return (glued[0, span] + glued[1, span]).reshape(NIF, PTS).astype(BF)

    def finish(g, c, n):
        tiles = [item(g, c + i) for i in range(n)]
        added = dot(link[g], tiles[0] if n == 1 else jnp.concatenate(tiles, axis=1))
        for i in range(n):
            at = g * NC + c + i
            out[at, 0:NIF] = (near[at] + added[:, i * PTS:(i + 1) * PTS]).astype(BF)

    def finish_pair(g, i, carry):
        finish(g, 2 * i, 2)
        return carry

    stores = []
    for g in range(2):
        lax.fori_loop(0, 9, functools.partial(finish_pair, g), 0)
        finish(g, 18, 1)
        block = pl.ds(g * NC, NC)
        fars[g].wait()
        stores.append(pltpu.make_async_copy(out.at[block], out_h.at[block], sems.at[5 + g]))
        stores[g].start()
    for store in stores:
        store.wait()


def body(modal, stiffness, mass, freq, coupling, route, target, contact_dof, evaluator, preload):
    slope_table, proj_table = fourier_tables()
    vmem = pl.BlockSpec(memory_space=pltpu.VMEM)
    anywhere = pl.BlockSpec(memory_space=pl.ANY)
    dma = pltpu.SemaphoreType.DMA
    part_f, part_b, got, got_tags = pl.pallas_call(
        main_kernel,
        out_shape=(
            jax.ShapeDtypeStruct((2 * NC, NIF, PTS), F32),
            jax.ShapeDtypeStruct((2 * NC, ND - NIF, PTS), BF),
            jax.ShapeDtypeStruct((NDEV, 64, PTS), BF),
            jax.ShapeDtypeStruct((NDEV, 1, 128), jnp.int32),
        ),
        in_specs=[anywhere] * 3 + [vmem] * 8,
        out_specs=(anywhere,) * 4,
        scratch_shapes=[
            pltpu.VMEM((2 * NC, 4, 32, PTS), BF),
            pltpu.VMEM((2 * NC, 12, 32, PTS), BF),
            pltpu.VMEM((2, ND, ND), BF),
            pltpu.VMEM((2, ND, ND), BF),
            pltpu.VMEM((NDEV, 128), jnp.int32),
            pltpu.SMEM((NDEV, 128), jnp.int32),
            pltpu.VMEM((NDEV, 1, 128), jnp.int32),
            pltpu.VMEM((NDEV, 64, PTS), BF),
            pltpu.VMEM((2, 4, 2, 20, 16, PTS), BF),
            pltpu.VMEM((2, 4, 2, 20, 16, PTS), BF),
            pltpu.VMEM((2, 4, 10, 16, PTS), BF),
            pltpu.VMEM((2, 4, 10, 16, PTS), BF),
            pltpu.VMEM((NZ, 4, 16, PTS), BF),
            pltpu.VMEM((NZ, 4, 16, PTS), BF),
            pltpu.VMEM((NZ, 4, 16, PTS), BF),
            pltpu.VMEM((2, 4, 10, 16, PTS), BF),
            pltpu.VMEM((2, 4, 2, 20, 16, PTS), BF),
            pltpu.VMEM((NC, 2 * ROWS, PTS), F32),
            pltpu.VMEM((NC, 2 * ROWS, PTS), F32),
            pltpu.VMEM((NC, 2 * ROWS, PTS), BF),
            pltpu.VMEM((2 * NC, ND, PTS), F32),
            pltpu.VMEM((2, 2 * ND, ND), BF),
            pltpu.VMEM((2, ND, 2 * ROWS), BF),
            pltpu.VMEM((2 * NC, NIF, PTS), F32),
            pltpu.VMEM((2 * NC, ND - NIF, PTS), BF),
            dma((9,)), dma, dma, dma, dma, dma((6,)), dma((6,)),
        ],
        compiler_params=pltpu.CompilerParams(
            collective_id=1, has_side_effects=True, vmem_limit_bytes=58 << 20
        ),
    )(modal.reshape(2 * NC, 16, 32, PTS), stiffness[0], mass[0], freq.reshape(1, PTS),
      preload, evaluator.reshape(1, ROWS), contact_dof, route.reshape(1, TILES), target,
      jnp.asarray(slope_table), jnp.asarray(proj_table))

    out = pl.pallas_call(
        last_kernel,
        out_shape=jax.ShapeDtypeStruct((2 * NC, ND, PTS), BF),
        in_specs=[anywhere] * 4 + [vmem],
        out_specs=anywhere,
        scratch_shapes=[
            pltpu.VMEM((NDEV, 64, PTS), BF),
            pltpu.SMEM((NDEV, 1, 128), jnp.int32),
            pltpu.VMEM((2 * NC, NIF, PTS), F32),
            pltpu.VMEM((2 * NC, ND, PTS), BF),
            pltpu.VMEM((2, TILES + 1, 32, PTS), F32),
            pltpu.VMEM((2, NIF, NIF), BF),
            dma((7,)),
        ],
        compiler_params=pltpu.CompilerParams(vmem_limit_bytes=58 << 20),
    )(got, got_tags, part_f, part_b, coupling[0])
    return out.reshape(1, 2, NC, ND, PTS)


def solution(mesh):
    placed = (
        P("section", "diam", None, None, None),
        P("section", "diam", None, None),
        P("section", "diam", None, None),
        P(),
        P("section", "diam", None, None, None),
        P("section", "diam", None),
        P("section", "diam"),
        P("section", "diam"),
        P("section", "diam", None),
        P("section", "diam"),
    )
    return jax.shard_map(
        body,
        mesh=mesh,
        in_specs=placed,
        out_specs=P("section", "diam", None, None, None),
        check_vma=False,
    )
```

time: 141 us -> 104 us (0.74)
  Pallas kernels: 122 us -> 104 us
  local copies, waits for them, and re-layouts: 13.8 us -> 0 us
  other arithmetic: 4.71 us -> 0 us
    pallas_call x1, Pallas kernels: 111 us -> 96.3 us  [body(): pl.pallas_call(main_kernel, out_shape=(jax.ShapeDtypeStruct((2 * NC, NIF,...]
    slice x1 -> x0, local copies, waits for them, and re-layouts: 5.73 us -> none  [body(): got_tags[:, :, 0]]
    unnamed x6 -> x0, local copies, waits for them, and re-layouts: 5.35 us -> none
    pallas_call x1, Pallas kernels: 10.9 us -> 8.05 us  [body(): pl.pallas_call(last_kernel, out_shape=jax.ShapeDtypeStruct((2 * NC, ND, P...]
    convert_element_type x3 -> x0, other arithmetic: 1.97 us -> none  [the longest x1 0.66 us: body(): contact_dof.astype(F32)]
where the time goes in v2:
time: 104 us
  Pallas kernels  104 us (100%)
    pallas_call x1, Pallas kernels, body(): pl.pallas_call(main_kernel, out_shape=(jax.ShapeDtypeStruct((2 * NC, NIF,...  96.3 us
    pallas_call x1, Pallas kernels, body(): pl.pallas_call(last_kernel, out_shape=jax.ShapeDtypeStruct((2 * NC, ND, P...  8.05 us

profile of v2, /device:TPU:4, one launch (start us, length us, event | category | flops | bytes accessed | tf_op | source)
XLA Modules:
  0.0 104.3 jit_solution(1046191785659879034)
XLA Ops:
  0.0 96.3 %shard_map.118 = (f32[38,128,128]{2,1,0:T(8,128)}, bf16[38,384,128]{2,1,0:T(8,128)(2,1)}, bf16[128,64,128]{2,1,0:T(8,128)(2,1)}, s32[128,1,128]{2,1,0:T(1,128)}) custom-call(bf16[38,16,32,128]{3,2,1,0:T(8,128)(2,1)} %bitcast.8, bf16[2,512,512]{2,1,0:T(8,128)(2,1)} %bitcast.9, bf16[2,512,512]{2,1,0:T(8,128)(2,1)} %bitcast.10, f32[1,128]{1,0:T(1,128)} %bitcast.13, ...), custom_call_target="tpu_custom_call" | custom-call | tf_op jit(solution)/shard_map/pallas_call | solution.py:477
  96.3 8.0 %shard_map.119 = bf16[38,512,128]{2,1,0:T(8,128)(2,1)} custom-call(bf16[128,64,128]{2,1,0:T(8,128)(2,1)} %get-tuple-element.9.got_h, s32[128,1,128]{2,1,0:T(1,128)} %get-tuple-element.10.tags_h, f32[38,128,128]{2,1,0:T(8,128)} %get-tuple-element.11.part_f, bf16[38,384,128]{2,1,0:T(8,128)(2,1)} %get-tuple-element.12.part_b, bf16[2,4,32,32]{3,2,1,0:T(8,128)(2,1)} %bitcast.11), custom_call_target="tpu_custom_call" | custom-call | tf_op jit(solution)/shard_map/pallas_call | solution.py:522

commit v3 on v2

--- a/solution.py
+++ b/solution.py
@@ -119,42 +119,6 @@
     tags[...] = jnp.bitwise_and(keys, 255).reshape(NDEV, 1, 128)
     listing = pltpu.make_async_copy(source, source_s, l_sem.at[4])
     listing.start()
-    listing.wait()
-    loads[0].wait()
-
-    def tile(t):
-        return edge[jnp.right_shift(t, 2), jnp.bitwise_and(t, 3)]
-
-    def pack(d, carry):
-        packed[d, 0:32, :] = tile(source_s[d, 0])
-        packed[d, 32:64, :] = tile(source_s[d, 64])
-        return carry
-
-    lax.fori_loop(0, NDEV, pack, 0)
-    pl.semaphore_wait(barrier, NDEV + NX + NY + NZ - 3)
-
-    def send_one(k):
-        px = lax.rem(x + k // (NZ * NY), NX)
-        pz = lax.rem(z + lax.rem(k, NZ), NZ)
-        py = lax.rem(y + lax.rem(k // NZ, NY), NY)
-        d = at(px, pz, py)
-        pltpu.make_async_remote_copy(
-            src_ref=tags.at[d], dst_ref=got_tags.at[me], send_sem=t_send, recv_sem=t_recv,
-            device_id=(other, d), device_id_type=MESH,
-        ).start()
-        pltpu.make_async_remote_copy(
-            src_ref=packed.at[d], dst_ref=got.at[me], send_sem=s_send, recv_sem=s_recv,
-            device_id=(other, d), device_id_type=MESH,
-        ).start()
-
-    def send_tiles(first, count):
-        def one(k, carry):
-            send_one(k)
-            return carry
-
-        lax.fori_loop(first, first + count, one, 0)
-
-    send_tiles(0, 24)
 
     pre_row = pre_ref[...].astype(F32)
     eval_row = eval_ref[...].astype(F32)
@@ -178,6 +142,7 @@
     load_hi = load.astype(BF)
     psend[1, :, :, 18] = load_hi.reshape(4, 2, 16, PTS)
     psend[1, :, :, 19] = (load - load_hi.astype(F32)).astype(BF).reshape(4, 2, 16, PTS)
+    loads[0].wait()
     loads[1].wait()
 
     def comps(g, c, n):
@@ -200,14 +165,14 @@
                 psend[half, :, :, (c + i) * 2 + a - 20 * half] = part
 
     def gather_pair(half, i, carry):
-        send_one(24 + 2 * i)
         gather(2 * i, 2, half)
-        send_one(25 + 2 * i)
         return carry
 
     lax.fori_loop(0, 5, functools.partial(gather_pair, 0), 0)
     lax.fori_loop(5, 9, functools.partial(gather_pair, 1), 0)
     gather(18, 1, 1)
+
+    pl.semaphore_wait(barrier, NDEV + NX + NY + NZ - 3)
 
     def push(src, dst, step, device):
         pltpu.make_async_remote_copy(
@@ -232,6 +197,40 @@
     for k in range(1, 4):
         for half in range(2):
             push(psend.at[half, peers[half][0](k)], rx.at[half, mine[half][0]], 0, device(half, 0, k))
+
+    listing.wait()
+
+    def tile(t):
+        return edge[jnp.right_shift(t, 2), jnp.bitwise_and(t, 3)]
+
+    def pack(d, carry):
+        packed[d, 0:32, :] = tile(source_s[d, 0])
+        packed[d, 32:64, :] = tile(source_s[d, 64])
+        return carry
+
+    lax.fori_loop(0, NDEV, pack, 0)
+    def send_one(k):
+        px = lax.rem(x + k // (NZ * NY), NX)
+        pz = lax.rem(z + lax.rem(k, NZ), NZ)
+        py = lax.rem(y + lax.rem(k // NZ, NY), NY)
+        d = at(px, pz, py)
+        pltpu.make_async_remote_copy(
+            src_ref=tags.at[d], dst_ref=got_tags.at[me], send_sem=t_send, recv_sem=t_recv,
+            device_id=(other, d), device_id_type=MESH,
+        ).start()
+        pltpu.make_async_remote_copy(
+            src_ref=packed.at[d], dst_ref=got.at[me], send_sem=s_send, recv_sem=s_recv,
+            device_id=(other, d), device_id_type=MESH,
+        ).start()
+
+    def send_tiles(first, count):
+        def one(k, carry):
+            send_one(k)
+            return carry
+
+        lax.fori_loop(first, first + count, one, 0)
+
+    send_tiles(0, 10)
     loads[2].wait()
     loads[3].wait()
     for g in range(2):
@@ -241,8 +240,8 @@
     soft = 0.01 / (freq[...] * freq[...])
 
     def contact(b, carry):
-        for i in range(3):
-            send_one(42 + 3 * b + i)
+        for i in range(2):
+            send_one(10 + 2 * b + i)
         low = pl.multiple_of(b * 8, 8)
         sides = []
         for a in range(2):
@@ -260,12 +259,13 @@
                 harm[c, pl.ds(a * ROWS + low, 8), :] = total[8 * c:8 * c + 8, a * PTS:(a + 1) * PTS]
         return carry
 
-    lax.fori_loop(0, 9, contact, 0)
+    lax.fori_loop(0, 8, contact, 0, unroll=2)
 
     def split(total):
         high = total.astype(BF)
         return high, (total - high.astype(F32)).astype(BF)
 
+    send_tiles(42, 4)
     arrived(rx.at[:, 0:3], 0)
     for half in range(2):
         whole = psend[half, mine[half][0]].astype(F32)
@@ -282,9 +282,10 @@
     for k in range(1, 4):
         for half in range(2):
             push(ysend.at[half, peers[half][1](k)], ry.at[half, mine[half][1]], 1, device(half, 1, k))
-    lax.fori_loop(9, 13, contact, 0)
+    lax.fori_loop(8, 12, contact, 0, unroll=2)
 
     odd = lax.rem(x, 2) == 1
+    send_tiles(46, 4)
     arrived(ry.at[:, 0:3], 1)
     zsend[5:8] = jnp.zeros((3, 4, 16, PTS), BF)
     for half in range(2):
@@ -299,7 +300,7 @@
             zsend[4, 3] = jnp.where(odd, low.astype(F32), whole[9]).astype(BF)
     for k in range(1, NZ):
         push(zsend.at[z_peer(k)], rz.at[z], 2, (sec, at(x, z_peer(k), y)))
-    lax.fori_loop(13, 16, contact, 0)
+    lax.fori_loop(12, 16, contact, 0, unroll=2)
 
     def balance(g, c, n):
         both = dot(stm[g], comps(g, c, n))
@@ -310,11 +311,13 @@
             resid[g * NC + c + i] = both[0:ND, lanes] - (scaled * scaled) * both[ND:2 * ND, lanes]
 
     def balance_pair(g, i, carry):
-        send_one(90 + 18 * g + 2 * i)
+        if g == 0:
+            send_one(62 + 2 * i)
+            send_one(63 + 2 * i)
         balance(g, 2 * i, 2)
-        send_one(91 + 18 * g + 2 * i)
-        return carry
-
+        return carry
+
+    send_tiles(50, 4)
     arrived(rz.at[0:7], 2)
     whole = zsend[z].astype(F32)
     for k in range(1, NZ):
@@ -328,6 +331,7 @@
         push(agz.at[z], agz.at[z], 3, (sec, at(x, z_peer(k), y)))
     lax.fori_loop(0, 5, functools.partial(balance_pair, 0), 0)
 
+    send_tiles(54, 4)
     arrived(agz.at[0:7], 3)
     for half in range(2):
         agy[half, mine[half][1]] = agz[0:5, 2 * half:2 * half + 2].reshape(10, 16, PTS)
@@ -337,15 +341,16 @@
     lax.fori_loop(5, 9, functools.partial(balance_pair, 0), 0)
     balance(0, 18, 1)
 
+    send_tiles(58, 4)
     arrived(agy.at[:, 0:3], 4)
     for half in range(2):
         agx[half, mine[half][0]] = agy[half].reshape(2, 20, 16, PTS)
         for k in range(1, 4):
             slot = agx.at[half, mine[half][0]]
             push(slot, slot, 5, device(half, 0, k))
-    lax.fori_loop(0, 9, functools.partial(balance_pair, 1), 0)
+    send_tiles(80, 48)
+    lax.fori_loop(0, 9, functools.partial(balance_pair, 1), 0, unroll=3)
     balance(1, 18, 1)
-    send_tiles(126, 2)
     arrived(agx.at[:, 0:3], 5)
 
     lane128 = lax.broadcasted_iota(jnp.int32, (ROWS, ROWS), 1).astype(F32)
@@ -369,8 +374,8 @@
             force[c, rows, :] = (STIFF * away + pressed * harm[c, rows, :]).astype(BF)
         return carry
 
-    lax.fori_loop(0, 10, functools.partial(forces, 0), 0)
-    lax.fori_loop(10, NC, functools.partial(forces, 1), 0)
+    lax.fori_loop(0, 10, functools.partial(forces, 0), 0, unroll=2)
+    lax.fori_loop(10, NC, functools.partial(forces, 1), 0, unroll=3)
 
     def finish(g, c, n):
         lines = [force[c + i] for i in range(n)]
@@ -387,7 +392,7 @@
 
     stores = []
     for g in range(2):
-        lax.fori_loop(0, 9, functools.partial(finish_pair, g), 0)
+        lax.fori_loop(0, 9, functools.partial(finish_pair, g), 0, unroll=3)
         finish(g, 18, 1)
         block = pl.ds(g * NC, NC)
         stores.append(pltpu.make_async_copy(far.at[block], part_b.at[block], l_sem.at[5 + g]))
@@ -459,7 +464,7 @@
 
     stores = []
     for g in range(2):
-        lax.fori_loop(0, 9, functools.partial(finish_pair, g), 0)
+        lax.fori_loop(0, 9, functools.partial(finish_pair, g), 0, unroll=3)
         finish(g, 18, 1)
         block = pl.ds(g * NC, NC)
         fars[g].wait()

time: 104 us -> 92.5 us (0.89)
  Pallas kernels: 104 us -> 92.1 us
    pallas_call x1, Pallas kernels: 96.3 us -> 85.5 us  [body(): pl.pallas_call(main_kernel, out_shape=(jax.ShapeDtypeStruct((2 * NC, NIF,...]
    pallas_call x1, Pallas kernels: 8.05 us -> 6.64 us  [body(): pl.pallas_call(last_kernel, out_shape=jax.ShapeDtypeStruct((2 * NC, ND, P...]
where the time goes in v3:
time: 92.5 us; the launch traced here: 92.1 us
  Pallas kernels  92.1 us (100%)
    pallas_call x1, Pallas kernels, body(): pl.pallas_call(main_kernel, out_shape=(jax.ShapeDtypeStruct((2 * NC, NIF,...  85.5 us
    pallas_call x1, Pallas kernels, body(): pl.pallas_call(last_kernel, out_shape=jax.ShapeDtypeStruct((2 * NC, ND, P...  6.64 us

profile of v3, /device:TPU:4, one launch (start us, length us, event | category | flops | bytes accessed | tf_op | source)
XLA Modules:
  0.0 92.1 jit_solution(17745273812284888887)
XLA Ops:
  0.0 85.5 %shard_map.118 = (f32[38,128,128]{2,1,0:T(8,128)}, bf16[38,384,128]{2,1,0:T(8,128)(2,1)}, bf16[128,64,128]{2,1,0:T(8,128)(2,1)}, s32[128,1,128]{2,1,0:T(1,128)}) custom-call(bf16[38,16,32,128]{3,2,1,0:T(8,128)(2,1)} %bitcast.8, bf16[2,512,512]{2,1,0:T(8,128)(2,1)} %bitcast.9, bf16[2,512,512]{2,1,0:T(8,128)(2,1)} %bitcast.10, f32[1,128]{1,0:T(1,128)} %bitcast.13, ...), custom_call_target="tpu_custom_call" | custom-call | tf_op jit(solution)/shard_map/pallas_call | solution.py:482
  85.5 6.6 %shard_map.119 = bf16[38,512,128]{2,1,0:T(8,128)(2,1)} custom-call(bf16[128,64,128]{2,1,0:T(8,128)(2,1)} %get-tuple-element.9.got_h, s32[128,1,128]{2,1,0:T(1,128)} %get-tuple-element.10.tags_h, f32[38,128,128]{2,1,0:T(8,128)} %get-tuple-element.11.part_f, bf16[38,384,128]{2,1,0:T(8,128)(2,1)} %get-tuple-element.12.part_b, bf16[2,4,32,32]{3,2,1,0:T(8,128)(2,1)} %bitcast.11), custom_call_target="tpu_custom_call" | custom-call | tf_op jit(solution)/shard_map/pallas_call | solution.py:527

commit v4 on v2

--- a/solution.py
+++ b/solution.py
@@ -61,7 +61,8 @@
     edge, inner, stiff, mass, source, source_s, tags, packed,
     psend, rx, ysend, ry, zsend, rz, agz, agy, agx,
     pay, harm, force, resid, stm, scat, near, far,
-    l_sem, s_send, s_recv, t_send, t_recv, r_send, r_recv,
+    relay, relay_tags,
+    l_sem, s_send, s_recv, t_send, t_recv, r_send, r_recv, z_send, z_recv, zt_send, zt_recv,
 ):
     sec = lax.axis_index("section")
     me = lax.axis_index("diam")
@@ -93,11 +94,9 @@
 
     barrier = pltpu.get_barrier_semaphore()
 
-    def hail(k, carry):
-        pl.semaphore_signal(barrier, inc=1, device_id=(other, k), device_id_type=MESH)
-        return carry
-
-    lax.fori_loop(0, NDEV, hail, 0)
+    for k in range(NX * NY):
+        there = at(x_peer(k // NY), z, y_peer(k % NY))
+        pl.semaphore_signal(barrier, inc=1, device_id=(other, there), device_id_type=MESH)
     for k in range(1, NX):
         pl.semaphore_signal(barrier, inc=1, device_id=(sec, at(x_peer(k), z, y)), device_id_type=MESH)
     for k in range(1, NY):
@@ -106,7 +105,13 @@
         pl.semaphore_signal(barrier, inc=1, device_id=(sec, at(x, z_peer(k), y)), device_id_type=MESH)
 
     spot = lax.broadcasted_iota(jnp.int32, (NDEV, TILES), 1)
-    named = route_ref[...] == lax.broadcasted_iota(jnp.int32, (NDEV, TILES), 0)
+    row = lax.broadcasted_iota(jnp.int32, (NDEV, TILES), 0)
+    inside = jnp.bitwise_and(row, 15)
+    owner = (
+        jnp.right_shift(inside, 2) * (NZ * NY) + jnp.right_shift(row, 4) * NY
+        + jnp.bitwise_and(inside, 3)
+    )
+    named = route_ref[...] == owner
     key = (spot * 256 + target_ref[...])
     first = jnp.min(jnp.where(named, key, 1 << 20), axis=1, keepdims=True)
     final = jnp.max(jnp.where(named, key, -1), axis=1, keepdims=True)
@@ -119,8 +124,9 @@
     tags[...] = jnp.bitwise_and(keys, 255).reshape(NDEV, 1, 128)
     listing = pltpu.make_async_copy(source, source_s, l_sem.at[4])
     listing.start()
+
+    loads[0].wait()
     listing.wait()
-    loads[0].wait()
 
     def tile(t):
         return edge[jnp.right_shift(t, 2), jnp.bitwise_and(t, 3)]
@@ -131,30 +137,24 @@
         return carry
 
     lax.fori_loop(0, NDEV, pack, 0)
-    pl.semaphore_wait(barrier, NDEV + NX + NY + NZ - 3)
-
-    def send_one(k):
-        px = lax.rem(x + k // (NZ * NY), NX)
-        pz = lax.rem(z + lax.rem(k, NZ), NZ)
-        py = lax.rem(y + lax.rem(k // NZ, NY), NY)
-        d = at(px, pz, py)
+    pl.semaphore_wait(barrier, NX * NY + NX + NY + NZ - 3)
+
+
+    def along(k):
+        to = z_peer(k)
+        chunk = pl.ds(16 * to, 16)
+        there = (sec, at(x, to, y))
         pltpu.make_async_remote_copy(
-            src_ref=tags.at[d], dst_ref=got_tags.at[me], send_sem=t_send, recv_sem=t_recv,
-            device_id=(other, d), device_id_type=MESH,
+            src_ref=tags.at[chunk], dst_ref=relay_tags.at[z], send_sem=zt_send,
+            recv_sem=zt_recv.at[k], device_id=there, device_id_type=MESH,
         ).start()
         pltpu.make_async_remote_copy(
-            src_ref=packed.at[d], dst_ref=got.at[me], send_sem=s_send, recv_sem=s_recv,
-            device_id=(other, d), device_id_type=MESH,
+            src_ref=packed.at[chunk], dst_ref=relay.at[z], send_sem=z_send,
+            recv_sem=z_recv.at[k], device_id=there, device_id_type=MESH,
         ).start()
 
-    def send_tiles(first, count):
-        def one(k, carry):
-            send_one(k)
-            return carry
-
-        lax.fori_loop(first, first + count, one, 0)
-
-    send_tiles(0, 24)
+    along(1)
+    along(7)
 
     pre_row = pre_ref[...].astype(F32)
     eval_row = eval_ref[...].astype(F32)
@@ -200,9 +200,7 @@
                 psend[half, :, :, (c + i) * 2 + a - 20 * half] = part
 
     def gather_pair(half, i, carry):
-        send_one(24 + 2 * i)
         gather(2 * i, 2, half)
-        send_one(25 + 2 * i)
         return carry
 
     lax.fori_loop(0, 5, functools.partial(gather_pair, 0), 0)
@@ -232,6 +230,36 @@
     for k in range(1, 4):
         for half in range(2):
             push(psend.at[half, peers[half][0](k)], rx.at[half, mine[half][0]], 0, device(half, 0, k))
+
+    def across(k):
+        origin = lax.rem(z + NZ - k, NZ)
+        if k:
+            pltpu.make_async_copy(relay_tags.at[0], relay_tags.at[0], zt_recv.at[k]).wait()
+            pltpu.make_async_copy(relay.at[0], relay.at[0], z_recv.at[k]).wait()
+        slot = at(x, origin, y)
+
+        def one(j, carry):
+            px, py = lax.rem(x + j // NY, NX), lax.rem(y + lax.rem(j, NY), NY)
+            d = at(px, z, py)
+            spot = px * NY + py
+            if k:
+                tag, tile = relay_tags.at[origin, spot], relay.at[origin, spot]
+            else:
+                tag, tile = tags.at[16 * z + spot], packed.at[16 * z + spot]
+            pltpu.make_async_remote_copy(
+                src_ref=tag, dst_ref=got_tags.at[slot], send_sem=t_send, recv_sem=t_recv,
+                device_id=(other, d), device_id_type=MESH,
+            ).start()
+            pltpu.make_async_remote_copy(
+                src_ref=tile, dst_ref=got.at[slot], send_sem=s_send, recv_sem=s_recv,
+                device_id=(other, d), device_id_type=MESH,
+            ).start()
+            return carry
+
+        lax.fori_loop(0, NX * NY, one, 0)
+
+    along(2)
+    along(6)
     loads[2].wait()
     loads[3].wait()
     for g in range(2):
@@ -241,8 +269,6 @@
     soft = 0.01 / (freq[...] * freq[...])
 
     def contact(b, carry):
-        for i in range(3):
-            send_one(42 + 3 * b + i)
         low = pl.multiple_of(b * 8, 8)
         sides = []
         for a in range(2):
@@ -260,7 +286,7 @@
                 harm[c, pl.ds(a * ROWS + low, 8), :] = total[8 * c:8 * c + 8, a * PTS:(a + 1) * PTS]
         return carry
 
-    lax.fori_loop(0, 9, contact, 0)
+    lax.fori_loop(0, 8, contact, 0, unroll=2)
 
     def split(total):
         high = total.astype(BF)
@@ -282,7 +308,7 @@
     for k in range(1, 4):
         for half in range(2):
             push(ysend.at[half, peers[half][1](k)], ry.at[half, mine[half][1]], 1, device(half, 1, k))
-    lax.fori_loop(9, 13, contact, 0)
+    lax.fori_loop(8, 12, contact, 0, unroll=2)
 
     odd = lax.rem(x, 2) == 1
     arrived(ry.at[:, 0:3], 1)
@@ -299,7 +325,10 @@
             zsend[4, 3] = jnp.where(odd, low.astype(F32), whole[9]).astype(BF)
     for k in range(1, NZ):
         push(zsend.at[z_peer(k)], rz.at[z], 2, (sec, at(x, z_peer(k), y)))
-    lax.fori_loop(13, 16, contact, 0)
+    across(0)
+    across(1)
+    across(7)
+    lax.fori_loop(12, 16, contact, 0, unroll=2)
 
     def balance(g, c, n):
         both = dot(stm[g], comps(g, c, n))
@@ -310,9 +339,7 @@
             resid[g * NC + c + i] = both[0:ND, lanes] - (scaled * scaled) * both[ND:2 * ND, lanes]
 
     def balance_pair(g, i, carry):
-        send_one(90 + 18 * g + 2 * i)
         balance(g, 2 * i, 2)
-        send_one(91 + 18 * g + 2 * i)
         return carry
 
     arrived(rz.at[0:7], 2)
@@ -326,6 +353,11 @@
     agz[z, 3] = jnp.where(here, low.astype(F32), whole[3]).astype(BF)
     for k in range(1, NZ):
         push(agz.at[z], agz.at[z], 3, (sec, at(x, z_peer(k), y)))
+    along(3)
+    along(5)
+    along(4)
+    across(2)
+    across(6)
     lax.fori_loop(0, 5, functools.partial(balance_pair, 0), 0)
 
     arrived(agz.at[0:7], 3)
@@ -343,9 +375,8 @@
         for k in range(1, 4):
             slot = agx.at[half, mine[half][0]]
             push(slot, slot, 5, device(half, 0, k))
-    lax.fori_loop(0, 9, functools.partial(balance_pair, 1), 0)
+    lax.fori_loop(0, 9, functools.partial(balance_pair, 1), 0, unroll=3)
     balance(1, 18, 1)
-    send_tiles(126, 2)
     arrived(agx.at[:, 0:3], 5)
 
     lane128 = lax.broadcasted_iota(jnp.int32, (ROWS, ROWS), 1).astype(F32)
@@ -369,8 +400,8 @@
             force[c, rows, :] = (STIFF * away + pressed * harm[c, rows, :]).astype(BF)
         return carry
 
-    lax.fori_loop(0, 10, functools.partial(forces, 0), 0)
-    lax.fori_loop(10, NC, functools.partial(forces, 1), 0)
+    lax.fori_loop(0, 10, functools.partial(forces, 0), 0, unroll=2)
+    lax.fori_loop(10, NC, functools.partial(forces, 1), 0, unroll=3)
 
     def finish(g, c, n):
         lines = [force[c + i] for i in range(n)]
@@ -387,7 +418,7 @@
 
     stores = []
     for g in range(2):
-        lax.fori_loop(0, 9, functools.partial(finish_pair, g), 0)
+        lax.fori_loop(0, 9, functools.partial(finish_pair, g), 0, unroll=3)
         finish(g, 18, 1)
         block = pl.ds(g * NC, NC)
         stores.append(pltpu.make_async_copy(far.at[block], part_b.at[block], l_sem.at[5 + g]))
@@ -395,6 +426,9 @@
         stores[-2].start()
         stores[-1].start()
 
+    across(3)
+    across(5)
+    across(4)
     left(rx.at[:, 0:3], 0)
     left(ry.at[:, 0:3], 1)
     left(rz.at[0:7], 2)
@@ -403,6 +437,8 @@
     left(agx.at[:, 0:3], 5)
     for store in stores:
         store.wait()
+    pltpu.make_async_copy(relay.at[0:7], relay.at[0:7], z_send).wait()
+    pltpu.make_async_copy(relay_tags.at[0:7], relay_tags.at[0:7], zt_send).wait()
     pltpu.make_async_copy(packed, packed, s_send).wait()
     pltpu.make_async_copy(tags, tags, t_send).wait()
     pltpu.make_async_copy(got_tags, got_tags, t_recv).wait()
@@ -459,7 +495,7 @@
 
     stores = []
     for g in range(2):
-        lax.fori_loop(0, 9, functools.partial(finish_pair, g), 0)
+        lax.fori_loop(0, 9, functools.partial(finish_pair, g), 0, unroll=3)
         finish(g, 18, 1)
         block = pl.ds(g * NC, NC)
         fars[g].wait()
@@ -510,7 +546,9 @@
             pltpu.VMEM((2, ND, 2 * ROWS), BF),
             pltpu.VMEM((2 * NC, NIF, PTS), F32),
             pltpu.VMEM((2 * NC, ND - NIF, PTS), BF),
-            dma((9,)), dma, dma, dma, dma, dma((6,)), dma((6,)),
+            pltpu.VMEM((NZ, 16, 64, PTS), BF),
+            pltpu.VMEM((NZ, 16, 1, 128), jnp.int32),
+            dma((9,)), dma, dma, dma, dma, dma((6,)), dma((6,)), dma, dma((NZ,)), dma, dma((NZ,)),
         ],
         compiler_params=pltpu.CompilerParams(
             collective_id=1, has_side_effects=True, vmem_limit_bytes=58 << 20

time: 104 us -> 84.3 us (0.81)
  the two profiles are of different devices: /device:TPU:4 before, /device:TPU:1 now
where the time goes in v4:
time: 84.3 us; the launch traced here: 84.1 us
  Pallas kernels  84.1 us (100%)
    pallas_call x1, Pallas kernels, body(): pl.pallas_call(main_kernel, out_shape=(jax.ShapeDtypeStruct((2 * NC, NIF,...  77.5 us
    pallas_call x1, Pallas kernels, body(): pl.pallas_call(last_kernel, out_shape=jax.ShapeDtypeStruct((2 * NC, ND, P...  6.64 us

profile of v4, /device:TPU:1, one launch (start us, length us, event | category | flops | bytes accessed | tf_op | source)
XLA Modules:
  0.0 84.1 jit_solution(126850943910520329)
XLA Ops:
  0.0 77.5 %shard_map.118 = (f32[38,128,128]{2,1,0:T(8,128)}, bf16[38,384,128]{2,1,0:T(8,128)(2,1)}, bf16[128,64,128]{2,1,0:T(8,128)(2,1)}, s32[128,1,128]{2,1,0:T(1,128)}) custom-call(bf16[38,16,32,128]{3,2,1,0:T(8,128)(2,1)} %bitcast.8, bf16[2,512,512]{2,1,0:T(8,128)(2,1)} %bitcast.9, bf16[2,512,512]{2,1,0:T(8,128)(2,1)} %bitcast.10, f32[1,128]{1,0:T(1,128)} %bitcast.13, ...), custom_call_target="tpu_custom_call" | custom-call | tf_op jit(solution)/shard_map/pallas_call | solution.py:513
  77.5 6.6 %shard_map.119 = bf16[38,512,128]{2,1,0:T(8,128)(2,1)} custom-call(bf16[128,64,128]{2,1,0:T(8,128)(2,1)} %get-tuple-element.9.got_h, s32[128,1,128]{2,1,0:T(1,128)} %get-tuple-element.10.tags_h, f32[38,128,128]{2,1,0:T(8,128)} %get-tuple-element.11.part_f, bf16[38,384,128]{2,1,0:T(8,128)(2,1)} %get-tuple-element.12.part_b, bf16[2,4,32,32]{3,2,1,0:T(8,128)(2,1)} %bitcast.11), custom_call_target="tpu_custom_call" | custom-call | tf_op jit(solution)/shard_map/pallas_call | solution.py:560

commit v5 on v4

--- a/solution.py
+++ b/solution.py
@@ -292,6 +292,7 @@
         high = total.astype(BF)
         return high, (total - high.astype(F32)).astype(BF)
 
+    along(4)
     arrived(rx.at[:, 0:3], 0)
     for half in range(2):
         whole = psend[half, mine[half][0]].astype(F32)
@@ -355,7 +356,6 @@
         push(agz.at[z], agz.at[z], 3, (sec, at(x, z_peer(k), y)))
     along(3)
     along(5)
-    along(4)
     across(2)
     across(6)
     lax.fori_loop(0, 5, functools.partial(balance_pair, 0), 0)
@@ -403,6 +403,8 @@
     lax.fori_loop(0, 10, functools.partial(forces, 0), 0, unroll=2)
     lax.fori_loop(10, NC, functools.partial(forces, 1), 0, unroll=3)
 
+    across(4)
+
     def finish(g, c, n):
         lines = [force[c + i] for i in range(n)]
         added = dot(scat[g], lines[0] if n == 1 else jnp.concatenate(lines, axis=1))
@@ -425,10 +427,10 @@
         stores.append(pltpu.make_async_copy(near.at[block], part_f.at[block], l_sem.at[7 + g]))
         stores[-2].start()
         stores[-1].start()
-
-    across(3)
+        if g == 0:
+            across(3)
+
     across(5)
-    across(4)
     left(rx.at[:, 0:3], 0)
     left(ry.at[:, 0:3], 1)
     left(rz.at[0:7], 2)

time: 84.3 us -> 89.8 us (1.065)
  Pallas kernels: 84.1 us -> 89.6 us
    pallas_call x1, Pallas kernels: 77.5 us -> 83 us  [body(): pl.pallas_call(main_kernel, out_shape=(jax.ShapeDtypeStruct((2 * NC, NIF,...]
where the time goes in v5:
time: 89.8 us; the launch traced here: 89.6 us
  Pallas kernels  89.6 us (100%)
    pallas_call x1, Pallas kernels, body(): pl.pallas_call(main_kernel, out_shape=(jax.ShapeDtypeStruct((2 * NC, NIF,...  83 us
    pallas_call x1, Pallas kernels, body(): pl.pallas_call(last_kernel, out_shape=jax.ShapeDtypeStruct((2 * NC, ND, P...  6.64 us

profile of v5, /device:TPU:1, one launch (start us, length us, event | category | flops | bytes accessed | tf_op | source)
XLA Modules:
  0.0 89.6 jit_solution(2449206755194029433)
XLA Ops:
  0.0 83.0 %shard_map.118 = (f32[38,128,128]{2,1,0:T(8,128)}, bf16[38,384,128]{2,1,0:T(8,128)(2,1)}, bf16[128,64,128]{2,1,0:T(8,128)(2,1)}, s32[128,1,128]{2,1,0:T(1,128)}) custom-call(bf16[38,16,32,128]{3,2,1,0:T(8,128)(2,1)} %bitcast.8, bf16[2,512,512]{2,1,0:T(8,128)(2,1)} %bitcast.9, bf16[2,512,512]{2,1,0:T(8,128)(2,1)} %bitcast.10, f32[1,128]{1,0:T(1,128)} %bitcast.13, ...), custom_call_target="tpu_custom_call" | custom-call | tf_op jit(solution)/shard_map/pallas_call | solution.py:515
  83.0 6.6 %shard_map.119 = bf16[38,512,128]{2,1,0:T(8,128)(2,1)} custom-call(bf16[128,64,128]{2,1,0:T(8,128)(2,1)} %get-tuple-element.9.got_h, s32[128,1,128]{2,1,0:T(1,128)} %get-tuple-element.10.tags_h, f32[38,128,128]{2,1,0:T(8,128)} %get-tuple-element.11.part_f, bf16[38,384,128]{2,1,0:T(8,128)(2,1)} %get-tuple-element.12.part_b, bf16[2,4,32,32]{3,2,1,0:T(8,128)(2,1)} %bitcast.11), custom_call_target="tpu_custom_call" | custom-call | tf_op jit(solution)/shard_map/pallas_call | solution.py:562
